TPU v7x, 32 devices: a whole 2x2x4 slice. The times are simulated.
32 devices in a mesh: img: 4 (over y, core), row: 2 (over x), col: 4 (over z).
Axes of the slice: x: 2, y: 2, z: 4, core: 2. Of those that a mesh axis runs over, the one named last changes fastest.
Arguments:
- image_tokens: bfloat16 [4, 64, 64, 768], P('img', 'row', 'col'), may hold values from -6 to 6
- cotangent: bfloat16 [4, 64, 64, 768], P('img', 'row', 'col'), may hold values from -6 to 6
- content_mask: int32 [4, 64, 64], P('img'), may hold values from 0 to 1, as said below
- norm1_gain: bfloat16 [768], P(('img', 'row', 'col')), may hold values from 0.25 to 1.75
- norm1_bias: bfloat16 [768], P(('img', 'row', 'col')), may hold values from -1.5 to 1.5
- qkv_weight: bfloat16 [768, 2304], P(('img', 'row', 'col')), may hold values from -0.21875 to 0.21875
- query_bias: bfloat16 [768], P(('img', 'row', 'col')), may hold values from -1.5 to 1.5
- value_bias: bfloat16 [768], P(('img', 'row', 'col')), may hold values from -1.5 to 1.5
- rel_rows: bfloat16 [27, 64], replicated, may hold values from -0.8984375 to 0.8984375
- rel_cols: bfloat16 [27, 64], replicated, may hold values from -0.8984375 to 0.8984375
- proj_weight: bfloat16 [768, 768], P(('img', 'row', 'col')), may hold values from -0.875 to 0.875
- proj_bias: bfloat16 [768], P(('img', 'row', 'col')), may hold values from -1.5 to 1.5
- norm2_gain: bfloat16 [768], P(('img', 'row', 'col')), may hold values from 0.25 to 1.75
- norm2_bias: bfloat16 [768], P(('img', 'row', 'col')), may hold values from -1.5 to 1.5
- fc1_weight: bfloat16 [768, 3072], P(('img', 'row', 'col')), may hold values from -0.21875 to 0.21875
- fc1_bias: bfloat16 [3072], P(('img', 'row', 'col')), may hold values from -1.5 to 1.5
- fc2_weight: bfloat16 [3072, 768], P(('img', 'row', 'col')), may hold values from -0.15625 to 0.15625
- fc2_bias: bfloat16 [768], P(('img', 'row', 'col')), may hold values from -1.5 to 1.5
Outputs:
- layer_out: bfloat16 [4, 64, 64, 768], P('img', 'row', 'col')
- grad_tokens: bfloat16 [4, 64, 64, 768], P('img', 'row', 'col')
- grad_norm1_gain: float32 [768], P(('img', 'row', 'col'))
- grad_norm1_bias: float32 [768], P(('img', 'row', 'col'))
- grad_qkv_weight: float32 [768, 2304], P(('img', 'row', 'col'))
- grad_query_bias: float32 [768], P(('img', 'row', 'col'))
- grad_value_bias: float32 [768], P(('img', 'row', 'col'))
- grad_rel_rows: float32 [27, 64], replicated
- grad_rel_cols: float32 [27, 64], replicated
- grad_proj_weight: float32 [768, 768], P(('img', 'row', 'col'))
- grad_proj_bias: float32 [768], P(('img', 'row', 'col'))
- grad_norm2_gain: float32 [768], P(('img', 'row', 'col'))
- grad_norm2_bias: float32 [768], P(('img', 'row', 'col'))
- grad_fc1_weight: float32 [768, 3072], P(('img', 'row', 'col'))
- grad_fc1_bias: float32 [3072], P(('img', 'row', 'col'))
- grad_fc2_weight: float32 [3072, 768], P(('img', 'row', 'col'))
- grad_fc2_bias: float32 [768], P(('img', 'row', 'col'))
Inputs may be any that keep to these rules, and one draw needn't show every extreme that they name: `content_mask`: each image's mask is 0 exactly on the cells whose row is at least its own bound tall and whose column is at least its own bound wide, and 1 elsewhere; tall and wide each lie between 57 and 64, so the first row and the first column are 1 throughout and the 0 cells may be none.
All inputs are finite; a program needn't handle non-finite values.
Results may differ from a plain program's by a relative error of at most 0.02.
Values may be sent and summed in bfloat16 or wider, within the bound.
A program may use at most 832 MiB of HBM per device.

v0:
```python
import jax
import jax.numpy as jnp
import numpy as np
from jax import lax
from jax.sharding import PartitionSpec as P

D = 768
HEADS = 12
HEAD_DIM = 64
WIN = 14


precise = lax.Precision.HIGHEST


def from_behind(value, axis, steps):
    count = lax.axis_size(axis)
    first, last = (max(0, -steps), min(count, count - steps))
    return lax.ppermute(value, axis, [(source, source + steps) for source in range(first, last)])


def for_sending(x):
    return jax.tree.map(lambda a: a.astype(jnp.bfloat16) if a.dtype == jnp.float32 else a, x)


def layer_norm(values, norm_gain, norm_shift):
    center = jnp.mean(values, axis=-1, keepdims=True)
    offset = values - center
    spread = jnp.mean(offset * offset, axis=-1, keepdims=True)
    return offset * lax.rsqrt(spread + 1e-06) * norm_gain + norm_shift


def gelu_exact(values):
    return jax.nn.gelu(values, approximate=False)


def rim_widths(tile_span):
    rim_reach = WIN - 1
    hop_count = -(-rim_reach // tile_span)
    offsets = list(range(hop_count, 0, -1)) + list(range(-1, -hop_count - 1, -1))
    widths = [min(tile_span, rim_reach - (abs(offset) - 1) * tile_span) for offset in offsets]
    return (hop_count, offsets, widths)


def extend(source, axis_dim):
    tile_span = source.shape[axis_dim]
    hop_count, offsets, widths = rim_widths(tile_span)
    received = []
    for number in range(len(offsets)):
        offset = offsets[number]
        if offset > 0:
            rim_piece = lax.slice_in_dim(
                source, tile_span - widths[number], tile_span, axis=axis_dim
            )
        else:
            rim_piece = lax.slice_in_dim(source, 0, widths[number], axis=axis_dim)
        if axis_dim == 1:
            arrived = from_behind(rim_piece, "row", offset)
        else:
            arrived = from_behind(rim_piece, "col", offset)
        received.append(arrived)
    return jnp.concatenate(received[:hop_count] + [source] + received[hop_count:], axis=axis_dim)


def retract(grad_wide, axis_dim, tile_span):
    hop_count, offsets, widths = rim_widths(tile_span)
    rim_reach = WIN - 1
    interior = lax.slice_in_dim(grad_wide, rim_reach, rim_reach + tile_span, axis=axis_dim)
    low_edge = 0
    high_edge = rim_reach + tile_span
    for number in range(len(offsets)):
        offset = offsets[number]
        rim_width = widths[number]
        padding = [(0, 0, 0)] * grad_wide.ndim
        if offset > 0:
            rim_piece = lax.slice_in_dim(grad_wide, low_edge, low_edge + rim_width, axis=axis_dim)
            low_edge = low_edge + rim_width
            padding[axis_dim] = (tile_span - rim_width, 0, 0)
        else:
            rim_piece = lax.slice_in_dim(grad_wide, high_edge, high_edge + rim_width, axis=axis_dim)
            high_edge = high_edge + rim_width
            padding[axis_dim] = (0, tile_span - rim_width, 0)
        if axis_dim == 1:
            returned = from_behind(for_sending(rim_piece), "row", -offset).astype(rim_piece.dtype)
        else:
            returned = from_behind(rim_piece.astype(jnp.bfloat16), "col", -offset).astype(
                rim_piece.dtype
            )
        interior = interior + lax.pad(returned, jnp.float32(0), padding)
    return interior


def window_slots(row_start, col_start, tile_rows, tile_cols):
    rim_reach = WIN - 1
    slots = []
    for slot_row in range((tile_rows - 1) // WIN + 2):
        for slot_col in range((tile_cols - 1) // WIN + 2):
            window_row = row_start // WIN + slot_row
            window_col = col_start // WIN + slot_col
            slot_live = (WIN * window_row < row_start + tile_rows) & (
                WIN * window_col < col_start + tile_cols
            )
            slots.append(
                (
                    WIN * window_row - row_start + rim_reach,
                    WIN * window_col - col_start + rim_reach,
                    slot_live.astype(jnp.float32),
                )
            )
    return slots


def cut_block(source, start_row, start_col):
    starts = (start_row, start_col) + (jnp.int32(0),) * (source.ndim - 2)
    return lax.dynamic_slice(source, starts, (WIN, WIN) + source.shape[2:])


def place_blocks(canvas, blocks, slots):
    for slot_index in range(len(slots)):
        entry = slots[slot_index]
        starts = (entry[0], entry[1]) + (jnp.int32(0),) * (canvas.ndim - 2)
        current = lax.dynamic_slice(canvas, starts, blocks.shape[1:])
        canvas = lax.dynamic_update_slice(canvas, current + blocks[slot_index], starts)
    return canvas


def slot_inputs(queries, wide_kv, key_valid, slots):
    rim_reach = WIN - 1
    tile_rows, tile_cols = (queries.shape[0], queries.shape[1])
    wide_q = jnp.pad(queries, ((rim_reach, rim_reach), (rim_reach, rim_reach), (0, 0)))
    owned = jnp.pad(jnp.ones((tile_rows, tile_cols), jnp.float32), rim_reach)
    q_slots = jnp.stack([cut_block(wide_q, entry[0], entry[1]) for entry in slots])
    kv_slots = jnp.stack([cut_block(wide_kv, entry[0], entry[1]) for entry in slots])
    key_ok = jnp.stack([cut_block(key_valid, entry[0], entry[1]) for entry in slots]).reshape(
        len(slots), WIN * WIN
    )
    own_slots = jnp.stack([cut_block(owned, entry[0], entry[1]) * entry[2] for entry in slots])
    return (q_slots, kv_slots, key_ok, own_slots)


def slot_scores(q_slots, kv_slots, key_ok, rows_win, cols_win):
    slot_count = q_slots.shape[0]
    q_heads = q_slots.reshape(slot_count, WIN, WIN, HEADS, HEAD_DIM)
    k_heads = kv_slots[:, :, :, 0].reshape(slot_count, WIN, WIN, HEADS, HEAD_DIM)
    raw_scores = jnp.einsum(
        "sxyhc,sabhc->shxyab", q_heads, k_heads, preferred_element_type=jnp.float32
    ) * HEAD_DIM ** (-0.5)
    along_rows = jnp.einsum(
        "sxyhc,xac->shxya", q_heads, rows_win, preferred_element_type=jnp.float32
    )
    along_cols = jnp.einsum(
        "sxyhc,ybc->shxyb", q_heads, cols_win, preferred_element_type=jnp.float32
    )
    scores = raw_scores + along_rows[:, :, :, :, :, None] + along_cols[:, :, :, :, None, :]
    scores = scores.reshape(slot_count, HEADS, WIN * WIN, WIN * WIN)
    return jnp.where(key_ok[:, None, None, :], scores, -1e30)


def attend_core(q_slots, kv_slots, key_ok, rows_win, cols_win):
    slot_count = q_slots.shape[0]
    scores = slot_scores(q_slots, kv_slots, key_ok, rows_win, cols_win)
    row_peak = jnp.max(scores, axis=-1, keepdims=True)
    exponent = jnp.exp(scores - row_peak)
    denominator = jnp.sum(exponent, axis=-1, keepdims=True)
    soft_b = (exponent / denominator).astype(jnp.bfloat16)
    v_heads = kv_slots[:, :, :, 1].reshape(slot_count, WIN * WIN, HEADS, HEAD_DIM)
    mixed_out = jnp.einsum("shqk,skhc->sqhc", soft_b, v_heads, preferred_element_type=jnp.float32)
    return (mixed_out.reshape(slot_count, WIN, WIN, D), row_peak + jnp.log(denominator))


def attend_back(q_slots, kv_slots, key_ok, grad_slots, log_total, rows_win, cols_win):
    slot_count = q_slots.shape[0]
    scale = HEAD_DIM ** (-0.5)
    g_heads = grad_slots.reshape(slot_count, WIN * WIN, HEADS, HEAD_DIM)
    q_heads = q_slots.reshape(slot_count, WIN * WIN, HEADS, HEAD_DIM)
    k_heads = kv_slots[:, :, :, 0].reshape(slot_count, WIN * WIN, HEADS, HEAD_DIM)
    v_heads = kv_slots[:, :, :, 1].reshape(slot_count, WIN * WIN, HEADS, HEAD_DIM)
    scores = slot_scores(q_slots, kv_slots, key_ok, rows_win, cols_win)
    soft = jnp.exp(scores - log_total)
    soft_b = soft.astype(jnp.bfloat16)
    d_soft = jnp.einsum("sqhc,skhc->shqk", g_heads, v_heads, preferred_element_type=jnp.float32)
    d_values = jnp.einsum("shqk,sqhc->skhc", soft_b, g_heads, preferred_element_type=jnp.float32)
    d_scores = (soft * (d_soft - jnp.sum(soft * d_soft, axis=-1, keepdims=True))).astype(
        jnp.bfloat16
    )
    d_queries = (
        jnp.einsum("shqk,skhc->sqhc", d_scores, k_heads, preferred_element_type=jnp.float32) * scale
    )
    d_keys = (
        jnp.einsum("shqk,sqhc->skhc", d_scores, q_heads, preferred_element_type=jnp.float32) * scale
    )
    grid_scores = d_scores.astype(jnp.float32).reshape(slot_count, HEADS, WIN, WIN, WIN, WIN)
    rows_sum = jnp.sum(grid_scores, axis=5)
    cols_sum = jnp.sum(grid_scores, axis=4)
    q_grid = q_slots.astype(jnp.float32).reshape(slot_count, WIN, WIN, HEADS, HEAD_DIM)
    d_rows_win = jnp.einsum("shxya,sxyhc->xac", rows_sum, q_grid, precision=precise)
    d_cols_win = jnp.einsum("shxyb,sxyhc->ybc", cols_sum, q_grid, precision=precise)
    d_queries = d_queries.reshape(slot_count, WIN, WIN, HEADS, HEAD_DIM)
    d_queries = d_queries + jnp.einsum(
        "shxya,xac->sxyhc", rows_sum, rows_win.astype(jnp.float32), precision=precise
    )
    d_queries = d_queries + jnp.einsum(
        "shxyb,ybc->sxyhc", cols_sum, cols_win.astype(jnp.float32), precision=precise
    )
    return (
        d_queries.reshape(slot_count, WIN, WIN, D),
        d_keys.reshape(slot_count, WIN, WIN, D),
        d_values.reshape(slot_count, WIN, WIN, D),
        d_rows_win,
        d_cols_win,
    )


def image_forward(queries, wide_kv, key_valid, slots, rows_win, cols_win):
    rim_reach = WIN - 1
    tile_rows, tile_cols = (queries.shape[0], queries.shape[1])
    q_slots, kv_slots, key_ok, own_slots = slot_inputs(queries, wide_kv, key_valid, slots)
    mixed_out, log_total = attend_core(q_slots, kv_slots, key_ok, rows_win, cols_win)
    mixed_out = mixed_out * own_slots[:, :, :, None]
    canvas = jnp.zeros((tile_rows + 2 * rim_reach, tile_cols + 2 * rim_reach, D), jnp.float32)
    canvas = place_blocks(canvas, mixed_out, slots)
    tile_out = canvas[rim_reach : rim_reach + tile_rows, rim_reach : rim_reach + tile_cols]
    return (tile_out, log_total)


def image_backward(queries, wide_kv, key_valid, grad_tile, log_total, slots, rows_win, cols_win):
    rim_reach = WIN - 1
    tile_rows, tile_cols = (queries.shape[0], queries.shape[1])
    q_slots, kv_slots, key_ok, own_slots = slot_inputs(queries, wide_kv, key_valid, slots)
    wide_grad = jnp.pad(grad_tile, ((rim_reach, rim_reach), (rim_reach, rim_reach), (0, 0)))
    grad_slots = jnp.stack([cut_block(wide_grad, entry[0], entry[1]) for entry in slots])
    grad_slots = grad_slots * own_slots[:, :, :, None].astype(jnp.bfloat16)
    d_queries, d_keys, d_values, d_rows_win, d_cols_win = attend_back(
        q_slots, kv_slots, key_ok, grad_slots, log_total, rows_win, cols_win
    )
    d_queries = d_queries * own_slots[:, :, :, None]
    q_canvas = jnp.zeros((tile_rows + 2 * rim_reach, tile_cols + 2 * rim_reach, D), jnp.float32)
    q_canvas = place_blocks(q_canvas, d_queries, slots)
    d_tile = q_canvas[rim_reach : rim_reach + tile_rows, rim_reach : rim_reach + tile_cols]
    d_kv = jnp.stack([d_keys, d_values], axis=3)
    kv_canvas = jnp.zeros((tile_rows + 2 * rim_reach, tile_cols + 2 * rim_reach, 2, D), jnp.float32)
    kv_canvas = place_blocks(kv_canvas, d_kv, slots)
    return (d_tile, kv_canvas, d_rows_win, d_cols_win)


def body(
    image_tokens,
    cotangent,
    content_mask,
    norm1_gain,
    norm1_bias,
    qkv_weight,
    query_bias,
    value_bias,
    rel_rows,
    rel_cols,
    proj_weight,
    proj_bias,
    norm2_gain,
    norm2_bias,
    fc1_weight,
    fc1_bias,
    fc2_weight,
    fc2_bias,
):
    images, tile_rows, tile_cols = (
        image_tokens.shape[0],
        image_tokens.shape[1],
        image_tokens.shape[2],
    )
    token_count = images * tile_rows * tile_cols
    rim_reach = WIN - 1
    gathered = (
        lax.all_gather(norm1_gain, ("img", "row", "col"), axis=0, tiled=True),
        lax.all_gather(norm1_bias, ("img", "row", "col"), axis=0, tiled=True),
        lax.all_gather(qkv_weight, ("img", "row", "col"), axis=0, tiled=True),
        lax.all_gather(query_bias, ("img", "row", "col"), axis=0, tiled=True),
        lax.all_gather(value_bias, ("img", "row", "col"), axis=0, tiled=True),
        lax.all_gather(proj_weight, ("img", "row", "col"), axis=0, tiled=True),
        lax.all_gather(proj_bias, ("img", "row", "col"), axis=0, tiled=True),
        lax.all_gather(norm2_gain, ("img", "row", "col"), axis=0, tiled=True),
        lax.all_gather(norm2_bias, ("img", "row", "col"), axis=0, tiled=True),
        lax.all_gather(fc1_weight, ("img", "row", "col"), axis=0, tiled=True),
        lax.all_gather(fc1_bias, ("img", "row", "col"), axis=0, tiled=True),
        lax.all_gather(fc2_weight, ("img", "row", "col"), axis=0, tiled=True),
        lax.all_gather(fc2_bias, ("img", "row", "col"), axis=0, tiled=True),
    )
    tokens = image_tokens.astype(jnp.float32).reshape(token_count, D)
    normed, norm1_pull = jax.vjp(
        layer_norm, tokens, gathered[0].astype(jnp.float32), gathered[1].astype(jnp.float32)
    )
    normed_b = normed.astype(jnp.bfloat16)
    mixed_qkv = jnp.dot(normed_b, gathered[2], preferred_element_type=jnp.float32)
    queries_flat = (mixed_qkv[:, :D] + gathered[3].astype(jnp.float32)).astype(jnp.bfloat16)
    keys_flat = mixed_qkv[:, D : 2 * D].astype(jnp.bfloat16)
    values_flat = (mixed_qkv[:, 2 * D :] + gathered[4].astype(jnp.float32)).astype(jnp.bfloat16)
    rel_index = np.arange(WIN)[:, None] - np.arange(WIN)[None, :] + WIN - 1
    rows_win = rel_rows[rel_index]
    cols_win = rel_cols[rel_index]
    queries = queries_flat.reshape(images, tile_rows, tile_cols, D)
    keyval = jnp.stack([keys_flat, values_flat], axis=1).reshape(images, tile_rows, tile_cols, 2, D)
    wide_kv = extend(extend(keyval, 1), 2)
    row_start = lax.axis_index("row") * tile_rows
    col_start = lax.axis_index("col") * tile_cols
    framed = jnp.pad(content_mask, ((0, 0), (rim_reach, rim_reach), (rim_reach, rim_reach)))
    key_valid = (
        lax.dynamic_slice(
            framed,
            (jnp.int32(0), row_start, col_start),
            (images, tile_rows + 2 * rim_reach, tile_cols + 2 * rim_reach),
        )
        == 1
    )
    slots = window_slots(row_start, col_start, tile_rows, tile_cols)
    attended, log_total = lax.map(
        lambda items: image_forward(items[0], items[1], items[2], slots, rows_win, cols_win),
        (queries, wide_kv, key_valid),
    )
    attended_b = attended.astype(jnp.bfloat16).reshape(token_count, D)
    residual = (
        tokens
        + jnp.dot(attended_b, gathered[5], preferred_element_type=jnp.float32)
        + gathered[6].astype(jnp.float32)
    )
    normed_two, norm2_pull = jax.vjp(
        layer_norm, residual, gathered[7].astype(jnp.float32), gathered[8].astype(jnp.float32)
    )
    normed_two_b = normed_two.astype(jnp.bfloat16)
    pre_gelu = jnp.dot(normed_two_b, gathered[9], preferred_element_type=jnp.float32) + gathered[
        10
    ].astype(jnp.float32)
    activated, gelu_pull = jax.vjp(gelu_exact, pre_gelu)
    activated_b = activated.astype(jnp.bfloat16)
    layer_out = (
        residual
        + jnp.dot(activated_b, gathered[11], preferred_element_type=jnp.float32)
        + gathered[12].astype(jnp.float32)
    )
    layer_out = layer_out.astype(jnp.bfloat16).reshape(image_tokens.shape)
    again = (
        lax.all_gather(qkv_weight, ("img", "row", "col"), axis=0, tiled=True),
        lax.all_gather(proj_weight, ("img", "row", "col"), axis=0, tiled=True),
        lax.all_gather(fc1_weight, ("img", "row", "col"), axis=0, tiled=True),
        lax.all_gather(fc2_weight, ("img", "row", "col"), axis=0, tiled=True),
    )
    grad_out = cotangent.reshape(token_count, D)
    grad_fc2_full = jnp.sum(grad_out.astype(jnp.float32), axis=0)
    grad_fc2_matrix = jnp.dot(activated_b.T, grad_out, preferred_element_type=jnp.float32)
    d_activated = jnp.dot(grad_out, again[3].T, preferred_element_type=jnp.float32)
    d_hidden_b = gelu_pull(d_activated)[0].astype(jnp.bfloat16)
    grad_fc1_full = jnp.sum(d_hidden_b.astype(jnp.float32), axis=0)
    grad_fc1_matrix = jnp.dot(normed_two_b.T, d_hidden_b, preferred_element_type=jnp.float32)
    d_normed_two = jnp.dot(d_hidden_b, again[2].T, preferred_element_type=jnp.float32)
    d_resid_norm, grad_gain_two, grad_shift_two = norm2_pull(d_normed_two)
    d_residual = grad_out.astype(jnp.float32) + d_resid_norm
    d_branch_b = d_residual.astype(jnp.bfloat16)
    grad_proj_full = jnp.sum(d_branch_b.astype(jnp.float32), axis=0)
    grad_proj_matrix = jnp.dot(attended_b.T, d_branch_b, preferred_element_type=jnp.float32)
    d_attended = jnp.dot(d_branch_b, again[1].T, preferred_element_type=jnp.float32).astype(
        jnp.bfloat16
    )
    d_attended_tiles = d_attended.reshape(images, tile_rows, tile_cols, D)
    d_queries, d_wide, d_rows_each, d_cols_each = lax.map(
        lambda items: image_backward(
            items[0], items[1], items[2], items[3], items[4], slots, rows_win, cols_win
        ),
        (queries, wide_kv, key_valid, d_attended_tiles, log_total),
    )
    d_keyval = retract(retract(d_wide, 2, tile_cols), 1, tile_rows)
    d_query_b = d_queries.astype(jnp.bfloat16).reshape(token_count, D)
    d_kv_b = d_keyval.astype(jnp.bfloat16).reshape(token_count, 2, D)
    d_mixed = jnp.concatenate([d_query_b, d_kv_b[:, 0], d_kv_b[:, 1]], axis=1)
    d_rows_total = jnp.sum(d_rows_each, axis=0)
    d_cols_total = jnp.sum(d_cols_each, axis=0)
    grad_query_full = jnp.sum(d_query_b.astype(jnp.float32), axis=0)
    grad_value_full = jnp.sum(d_mixed[:, 2 * D :].astype(jnp.float32), axis=0)
    grad_qkv_matrix = jnp.dot(normed_b.T, d_mixed, preferred_element_type=jnp.float32)
    d_normed = jnp.dot(d_mixed, again[0].T, preferred_element_type=jnp.float32)
    d_tokens_norm, grad_gain_one, grad_shift_one = norm1_pull(d_normed)
    grad_tokens = (d_residual + d_tokens_norm).astype(jnp.bfloat16).reshape(image_tokens.shape)
    rel_table = (rel_index[:, :, None] == np.arange(2 * WIN - 1)[None, None, :]).astype(np.float32)
    local_rows = jnp.einsum("xaj,xac->jc", rel_table, d_rows_total, precision=precise)
    local_cols = jnp.einsum("ybj,ybc->jc", rel_table, d_cols_total, precision=precise)
    grad_rel_rows, grad_rel_cols = lax.psum((local_rows, local_cols), ("img", "row", "col"))
    full_grads = [
        grad_gain_one,
        grad_shift_one,
        grad_qkv_matrix,
        grad_query_full,
        grad_value_full,
        grad_proj_matrix,
        grad_proj_full,
        grad_gain_two,
        grad_shift_two,
        grad_fc1_matrix,
        grad_fc1_full,
        grad_fc2_matrix,
        grad_fc2_full,
    ]
    shard_shapes = [
        norm1_gain.shape,
        norm1_bias.shape,
        qkv_weight.shape,
        query_bias.shape,
        value_bias.shape,
        proj_weight.shape,
        proj_bias.shape,
        norm2_gain.shape,
        norm2_bias.shape,
        fc1_weight.shape,
        fc1_bias.shape,
        fc2_weight.shape,
        fc2_bias.shape,
    ]
    groups = lax.axis_size("img")
    grouped = [
        member.reshape((groups, member.shape[0] // groups) + member.shape[1:])
        for member in full_grads
    ]
    partial_sums = (
        lax.psum_scatter(
            grouped[0].astype(jnp.bfloat16), ("row", "col"), scatter_dimension=1, tiled=True
        ).astype(jnp.float32),
        lax.psum_scatter(
            grouped[1].astype(jnp.bfloat16), ("row", "col"), scatter_dimension=1, tiled=True
        ).astype(jnp.float32),
        lax.psum_scatter(
            grouped[2].astype(jnp.bfloat16), ("row", "col"), scatter_dimension=1, tiled=True
        ).astype(jnp.float32),
        lax.psum_scatter(
            grouped[3].astype(jnp.bfloat16), ("row", "col"), scatter_dimension=1, tiled=True
        ).astype(jnp.float32),
        lax.psum_scatter(
            grouped[4].astype(jnp.bfloat16), ("row", "col"), scatter_dimension=1, tiled=True
        ).astype(jnp.float32),
        lax.psum_scatter(
            grouped[5].astype(jnp.bfloat16), ("row", "col"), scatter_dimension=1, tiled=True
        ).astype(jnp.float32),
        lax.psum_scatter(
            grouped[6].astype(jnp.bfloat16), ("row", "col"), scatter_dimension=1, tiled=True
        ).astype(jnp.float32),
        lax.psum_scatter(
            grouped[7].astype(jnp.bfloat16), ("row", "col"), scatter_dimension=1, tiled=True
        ).astype(jnp.float32),
        lax.psum_scatter(
            grouped[8].astype(jnp.bfloat16), ("row", "col"), scatter_dimension=1, tiled=True
        ).astype(jnp.float32),
        lax.psum_scatter(
            grouped[9].astype(jnp.bfloat16), ("row", "col"), scatter_dimension=1, tiled=True
        ).astype(jnp.float32),
        lax.psum_scatter(
            grouped[10].astype(jnp.bfloat16), ("row", "col"), scatter_dimension=1, tiled=True
        ).astype(jnp.float32),
        lax.psum_scatter(
            grouped[11].astype(jnp.bfloat16), ("row", "col"), scatter_dimension=1, tiled=True
        ).astype(jnp.float32),
        lax.psum_scatter(
            grouped[12].astype(jnp.bfloat16), ("row", "col"), scatter_dimension=1, tiled=True
        ).astype(jnp.float32),
    )
    summed = (
        lax.psum_scatter(
            partial_sums[0].astype(jnp.bfloat16), "img", scatter_dimension=0, tiled=True
        ).astype(jnp.float32),
        lax.psum_scatter(
            partial_sums[1].astype(jnp.bfloat16), "img", scatter_dimension=0, tiled=True
        ).astype(jnp.float32),
        lax.psum_scatter(
            partial_sums[2].astype(jnp.bfloat16), "img", scatter_dimension=0, tiled=True
        ).astype(jnp.float32),
        lax.psum_scatter(
            partial_sums[3].astype(jnp.bfloat16), "img", scatter_dimension=0, tiled=True
        ).astype(jnp.float32),
        lax.psum_scatter(
            partial_sums[4].astype(jnp.bfloat16), "img", scatter_dimension=0, tiled=True
        ).astype(jnp.float32),
        lax.psum_scatter(
            partial_sums[5].astype(jnp.bfloat16), "img", scatter_dimension=0, tiled=True
        ).astype(jnp.float32),
        lax.psum_scatter(
            partial_sums[6].astype(jnp.bfloat16), "img", scatter_dimension=0, tiled=True
        ).astype(jnp.float32),
        lax.psum_scatter(
            partial_sums[7].astype(jnp.bfloat16), "img", scatter_dimension=0, tiled=True
        ).astype(jnp.float32),
        lax.psum_scatter(
            partial_sums[8].astype(jnp.bfloat16), "img", scatter_dimension=0, tiled=True
        ).astype(jnp.float32),
        lax.psum_scatter(
            partial_sums[9].astype(jnp.bfloat16), "img", scatter_dimension=0, tiled=True
        ).astype(jnp.float32),
        lax.psum_scatter(
            partial_sums[10].astype(jnp.bfloat16), "img", scatter_dimension=0, tiled=True
        ).astype(jnp.float32),
        lax.psum_scatter(
            partial_sums[11].astype(jnp.bfloat16), "img", scatter_dimension=0, tiled=True
        ).astype(jnp.float32),
        lax.psum_scatter(
            partial_sums[12].astype(jnp.bfloat16), "img", scatter_dimension=0, tiled=True
        ).astype(jnp.float32),
    )
    shards = [summed[number].reshape(shard_shapes[number]) for number in range(len(shard_shapes))]
    return (
        layer_out,
        grad_tokens,
        shards[0],
        shards[1],
        shards[2],
        shards[3],
        shards[4],
        grad_rel_rows,
        grad_rel_cols,
        shards[5],
        shards[6],
        shards[7],
        shards[8],
        shards[9],
        shards[10],
        shards[11],
        shards[12],
    )


def solution(mesh):
    in_specs = (
        P("img", "row", "col", None),
        P("img", "row", "col", None),
        P("img", None, None),
        P(("img", "row", "col")),
        P(("img", "row", "col")),
        P(("img", "row", "col"), None),
        P(("img", "row", "col")),
        P(("img", "row", "col")),
        P(),
        P(),
        P(("img", "row", "col"), None),
        P(("img", "row", "col")),
        P(("img", "row", "col")),
        P(("img", "row", "col")),
        P(("img", "row", "col"), None),
        P(("img", "row", "col")),
        P(("img", "row", "col"), None),
        P(("img", "row", "col")),
    )
    out_specs = (
        P("img", "row", "col", None),
        P("img", "row", "col", None),
        P(("img", "row", "col")),
        P(("img", "row", "col")),
        P(("img", "row", "col"), None),
        P(("img", "row", "col")),
        P(("img", "row", "col")),
        P(),
        P(),
        P(("img", "row", "col"), None),
        P(("img", "row", "col")),
        P(("img", "row", "col")),
        P(("img", "row", "col")),
        P(("img", "row", "col"), None),
        P(("img", "row", "col")),
        P(("img", "row", "col"), None),
        P(("img", "row", "col")),
    )
    return jax.shard_map(body, mesh=mesh, in_specs=in_specs, out_specs=out_specs, check_vma=False)
```

profile of v0, /device:TPU:0, one launch (start us, length us, event | category | flops | bytes accessed | tf_op | source)
XLA Modules:
  0.0 2266.4 jit_solution(1265006526556800649)
XLA Ops:
  20.6 43.3 %all-reduce.35 = (bf16[768]{0:T(1024)(128)(2,1)S(1)}, bf16[768]{0:T(1024)(128)(2,1)S(1)}, bf16[768]{0:T(1024)(128)(2,1)S(1)}, bf16[768]{0:T(1024)(128)(2,1)S(1)}...) all-reduce(bf16[768]{0:T(1024)(128)(2,1)S(1)} %dynamic-update-slice, ...), channel_id=1, replica_groups=mesh['img'=4,'row'=2,'col'=4] {'img','row','col'}, use_global_device_ids=true, to_apply=%add.9 | all-reduce | flops 9216 | bytes 36864
  148.1 6.2 pad_maximum_fusion.1
  165.9 11.7 fusion.20
  202.9 20.0 copy.170
  222.9 11.3 fusion.23
  234.2 20.5 copy.172
  290.9 40.7 %pad_maximum_fusion = bf16[1,58,42,2,768]{4,3,2,1,0:T(2,128)(2,1)S(1)} fusion(bf16[1,58,13,2,768]{4,3,2,1,0:T(2,128)(2,1)} %collective-permute-done.3, bf16[1,13,16,2,768]{4,3,2,1,0:T(2,128)(2,1)} %collective-permute-done.1, bf16[1,32,16,1,768]{4,3,2,1,0:T(2,128)(2,1)S(1)} %copy.155, bf16[1,32,16,1,768]{4,3,2,1,0:T(2,128)(2,1)S(1)} %copy.154, ...), kind=kLoop, calls=%fused_computation.60 | loop fusion | flops 44900352 | bytes 14966784 | tf_op jit(solution)/shard_map/concatenate | solution.py:62
  337.6 40.4 %slice_reduce_fusion = (bf16[12,14,14,768]{3,2,1,0:T(8,128)(2,1)}, bf16[12,14,14,768]{3,2,1,0:T(8,128)(2,1)}) fusion(bf16[12,14,14,2,768]{4,3,2,1,0:T(2,128)(2,1)S(1)} %dynamic-slice_dynamic-update-slice_fusion), kind=kLoop, calls=%fused_computation.63 | loop fusion | bytes 14450688 | tf_op jit(solution)/shard_map/while/body/eval_jaxpr/slice | solution.py:144
  377.9 12.6 squeeze.236
  390.5 99.1 %select_reduce_fusion = (f32[12,12,14,14]{3,2,1,0:T(8,128)S(1)}, f32[12,12,14,14,14,14]{3,5,4,2,1,0:T(8,128)}) fusion(pred[12,14,14]{2,1,0:T(8,128)(4,1)S(1)} %copy-done.66, f32[12,12,14,14,14]{3,4,2,1,0:T(8,128)} %copy.172, f32[12,12,14,14,14]{3,4,2,1,0:T(8,128)} %copy.170, bf16[12,14,14,12,64,1]{4,3,2,1,0,5:T(8,128)(2,1)} %bitcast.509, ...), kind=kOutput, calls=%fused_computation.4 | convolution fusion | flops 735715008 | bytes 32629296 | tf_op jit(solution)/shard_map/while/body/eval_jaxpr/sxyhc,sabhc->shxyab/dot_general | solution.py:145
  489.6 218.6 %copy.255 = f32[12,12,14,14,14,14]{3,2,5,4,1,0:T(8,128)} copy(f32[12,12,14,14,14,14]{3,5,4,2,1,0:T(8,128)} %get-tuple-element.557) | data formatting | bytes 44255232 | tf_op jit(solution)/shard_map/while/body/eval_jaxpr/reshape | solution.py:155
  708.2 81.8 %exponential_reduce_fusion = f32[12,12,14,14]{3,2,1,0:T(8,128)S(1)} fusion(f32[12,12,14,14,14,14]{3,5,4,2,1,0:T(8,128)} %get-tuple-element.557, f32[12,12,14,14]{3,2,1,0:T(8,128)S(1)} %get-tuple-element.556, pred[12,14,14]{2,1,0:T(8,128)(4,1)S(1)} %copy-done.66), kind=kLoop, calls=%fused_computation.2 | loop fusion | flops 16567488 | bytes 22355760 | tf_op jit(solution)/shard_map/while/body/eval_jaxpr/reduce_sum | solution.py:164
  790.9 130.0 %reshape.926 = f32[12,12,196,196]{2,3,1,0:T(8,128)} reshape(f32[12,12,14,14,14,14]{3,2,5,4,1,0:T(8,128)} %copy.255) | data formatting | bytes 44255232 | tf_op jit(solution)/shard_map/while/body/eval_jaxpr/reshape | solution.py:155
  920.9 12.6 squeeze.234
  933.5 12.4 copy.175
  945.9 17.3 fusion.57
  963.2 17.6 copy.177
  980.8 16.3 reshape.810
  1087.7 20.2 fusion.33
  1107.9 20.1 fusion.204
  1192.8 27.0 %multiply_reduce_fusion = (f32[12,12,196]{2,1,0:T(8,128)S(1)}, f32[12,12,196,196]{2,3,1,0:T(8,128)}) fusion(f32[12,12,196,196]{2,3,1,0:T(8,128)} %reshape.926, f32[12,12,196]{2,1,0:T(8,128)S(1)} %log_add_fusion, pred[12,196]{1,0:T(8,128)(4,1)S(1)} %bitcast.534, bf16[12,196,12,64]{1,3,2,0:T(8,128)(2,1)} %copy.175, ...), kind=kOutput, calls=%fused_computation.6 | convolution fusion | flops 731989440 | bytes 51713424 | tf_op jit(solution)/shard_map/while/body/eval_jaxpr/sqhc,skhc->shqk/dot_general | solution.py:181
  1219.8 25.0 %multiply_convert_fusion = bf16[12,12,196,196]{2,3,1,0:T(8,128)(2,1)} fusion(f32[12,12,196,196]{2,3,1,0:T(8,128)} %get-tuple-element.562, f32[12,12,196,196]{2,3,1,0:T(8,128)} %reshape.926, f32[12,12,196]{2,1,0:T(8,128)S(1)} %get-tuple-element.561, f32[12,12,196]{2,1,0:T(8,128)S(1)} %log_add_fusion, pred[12,196]{1,0:T(8,128)(4,1)S(1)} %bitcast.535), kind=kLoop, calls=%fused_computation.5 | loop fusion | flops 27659520 | bytes 55547184 | tf_op jit(solution)/shard_map/while/body/eval_jaxpr/convert_element_type | solution.py:183
  1244.8 123.8 %reshape.850 = f32[12,12,14,14,14,14]{3,2,5,4,1,0:T(8,128)} reshape(bf16[12,12,196,196]{2,3,1,0:T(8,128)(2,1)} %multiply_convert_fusion) | data formatting | bytes 33191424 | tf_op jit(solution)/shard_map/while/body/eval_jaxpr/reshape | solution.py:192
  1375.0 6.7 convolution_convert_fusion.2
  1381.7 102.4 %fusion.202 = (f32[12,12,14,14,14]{3,2,4,1,0:T(8,128)}, f32[12,12,14,14,14]{3,2,4,1,0:T(8,128)}) fusion(f32[12,12,14,14,14,14]{3,2,5,4,1,0:T(8,128)} %reshape.850), kind=kLoop, calls=%fused_computation.442 | loop fusion | flops 10273536 | bytes 25288704 | tf_op jit(solution)/shard_map/while/body/eval_jaxpr/reduce_sum | solution.py:193
  1484.1 12.7 squeeze.249
  1509.6 23.0 %copy.196 = f32[12,12,14,14,14]{4,2,1,0,3:T(8,128)} copy(f32[12,12,14,14,14]{3,2,4,1,0:T(8,128)} %get-tuple-element.434) | data formatting | bytes 3161088 | tf_op jit(solution)/shard_map/while/body/eval_jaxpr/reduce_sum | solution.py:194
  1532.6 15.4 multiply_bitcast_fusion.1
  1548.1 12.2 copy.193
  1560.3 16.4 reshape.814
  1576.7 17.0 fusion.58
  1593.7 17.6 copy.214
  1611.3 16.3 reshape.820
  1627.6 11.1 multiply_bitcast_fusion
  1638.7 17.6 copy.212
  1656.3 16.3 reshape.819
  1686.6 14.8 fusion.134
  1701.4 8.1 broadcast.235
  1709.5 8.9 dynamic_update_slice.221
  1718.3 30.5 %bitcast_add_fusion = f32[12,14,14,12,64]{4,2,3,0,1:T(8,128)S(1)} fusion(f32[14,12,12,14,64]{4,3,2,1,0:T(8,128)} %fusion.134, f32[12,14,14,12,64]{4,2,1,3,0:T(8,128)} %reshape.814, f32[12,12,14,14,14]{3,2,4,1,0:T(8,128)} %get-tuple-element.433, bf16[14,14,64,1,1]{2,1,0,3,4:T(8,128)(2,1)S(1)} %copy-done.49), kind=kOutput, calls=%fused_computation.36 | convolution fusion | flops 307077120 | bytes 23281664 | tf_op jit(solution)/shard_map/while/body/eval_jaxpr/shxya,xac->sxyhc/dot_general | solution.py:199
  1751.1 10.8 copy.198
  1761.9 16.3 reshape.817
  1778.3 8.2 dynamic_update_slice.222
  1788.7 8.3 dynamic_update_slice.223
  1799.3 8.5 dynamic_update_slice.224
  1810.0 8.2 dynamic_update_slice.225
  1820.5 8.2 dynamic_update_slice.226
  1831.0 8.4 dynamic_update_slice.227
  1841.7 8.2 dynamic_update_slice.228
  1852.1 8.2 dynamic_update_slice.229
  1862.6 8.5 dynamic_update_slice.230
  1873.3 8.0 dynamic_update_slice.231
  1883.5 8.0 dynamic_update_slice.232
  1891.5 6.4 convert.107
  1907.0 6.8 collective-permute-start.5
  1991.1 6.2 fusion.209
  1998.7 7.1 collective-permute-start.7
  2033.7 23.5 %copy.250 = f32[12,12,14,14,14]{2,4,0,1,3:T(8,128)} copy(f32[12,12,14,14,14]{3,2,4,1,0:T(8,128)} %get-tuple-element.434) | data formatting | bytes 3161088 | tf_op jit(solution)/shard_map/while/body/eval_jaxpr/reduce_sum | solution.py:194
  2057.5 21.0 fusion.99
  2078.8 23.9 %fusion.102 = f32[14,14,64]{2,1,0:T(8,128)S(1)} fusion(bf16[12,14,14,12,64]{4,2,1,3,0:T(8,128)(2,1)} %copy_dynamic-update-slice_fusion, f32[12,12,14,14,14]{3,2,4,1,0:T(8,128)} %get-tuple-element.433), kind=kOutput, calls=%fused_computation.185 | convolution fusion | flops 303464448 | bytes 5243392 | tf_op jit(solution)/shard_map/while/body/eval_jaxpr/shxya,sxyhc->xac/dot_general | solution.py:196
  2103.0 40.2 %all-reduce.34 = (f32[27,64]{1,0:T(8,128)}, f32[27,64]{1,0:T(8,128)}) all-reduce(f32[27,64]{1,0:T(8,128)S(1)} %convolution_bitcast_fusion.1, f32[27,64]{1,0:T(8,128)S(1)} %convolution_bitcast_fusion), channel_id=1, replica_groups=mesh['img'=4,'row'=2,'col'=4] {'img','row','col'}, use_global_device_ids=true, to_apply=%region_27.28 | all-reduce | flops 3456 | bytes 27648 | tf_op jit(solution)/shard_map/psum | solution.py:384
  2143.2 9.6 add_convert_fusion.2
  2163.7 37.0 %all-reduce.36 = (bf16[4,192]{1,0:T(4,128)(2,1)S(1)}, bf16[4,192]{1,0:T(4,128)(2,1)S(1)}, bf16[4,192]{1,0:T(4,128)(2,1)S(1)}, bf16[4,192]{1,0:T(4,128)(2,1)S(1)}...) all-reduce(bf16[4,192]{1,0:T(4,128)(2,1)S(1)} %convert_element_type, ...), channel_id=2, replica_groups=mesh['img'=4,'row'=2,'col'=4] {'row','col'}, use_global_device_ids=true, to_apply=%region_14.15.clone | all-reduce | flops 6144 | bytes 24576
  2236.0 22.0 reduce-scatter.26.cloned.1.call-done
  (592 shorter events, 552.7 us)
Async XLA Ops:
  7.2 58.1 %copy-start = (bf16[27,64]{1,0:T(8,128)(2,1)S(1)}, bf16[27,64]{1,0:T(8,128)(2,1)}, u32[]{:S(2)}) copy-start(bf16[27,64]{1,0:T(8,128)(2,1)} %param.31) | copy-start | bytes 10372
  7.2 74.2 %all-gather.5.cloned.1.call-start = ((), (), s32[]{:S(2)}) async-start(), calls=%async_computation.9 | async-start | bytes 3649536 | tf_op jit(solution)/shard_map/all_gather | solution.py:276
  7.9 1076.3 %all-gather.7.cloned.1.call-start = ((), (), s32[]{:S(2)}) async-start(), calls=%async_computation.10 | async-start | bytes 1216512 | tf_op jit(solution)/shard_map/all_gather | solution.py:279
  8.7 1079.0 %all-gather.9.cloned.1.call-start = ((), (), s32[]{:S(2)}) async-start(), calls=%async_computation.11 | async-start | bytes 4866048 | tf_op jit(solution)/shard_map/all_gather | solution.py:283
  9.4 1098.5 %all-gather.11.cloned.1.call-start = ((), (), s32[]{:S(2)}) async-start(), calls=%async_computation.12 | async-start | bytes 4866048 | tf_op jit(solution)/shard_map/all_gather | solution.py:285
  10.0 1363.2 %reduce-scatter.38.cloned.1.call-start = ((), (), s32[]{:S(2)}) async-start(), calls=%async_computation.19 | async-start | bytes 1327104
  12.9 72.5 %copy-start.61 = (f32[512]{0:T(512)}, f32[512]{0:T(512)S(1)}, u32[]{:S(2)}) copy-start(f32[512]{0:T(512)S(1)} %div.85) | copy-start | bytes 6148
  63.9 21.5 copy-start.59
  64.0 21.5 copy-start.63
  68.1 154.7 %copy-start.46 = (bf16[14,14,64,1,1]{2,1,0,3,4:T(8,128)(2,1)}, bf16[14,14,64,1,1]{2,1,0,3,4:T(8,128)(2,1)S(1)}, u32[]{:S(2)}) copy-start(bf16[14,14,64,1,1]{2,1,0,3,4:T(8,128)(2,1)S(1)} %reshape.916) | copy-start | bytes 75268
  92.5 20.5 copy-start.28
  92.5 20.5 copy-start.29
  92.5 20.5 copy-start.30
  92.5 20.5 copy-start.31
  92.5 49.9 %copy-start.25 = (bf16[14,14,768]{2,1,0:T(8,128)(2,1)}, bf16[14,14,768]{2,1,0:T(8,128)(2,1)S(1)}, u32[]{:S(2)}) copy-start(bf16[14,14,768]{2,1,0:T(8,128)(2,1)S(1)} %get-tuple-element.532) | copy-start | bytes 903172
  113.0 19.4 copy-start.24
  113.0 20.5 copy-start.23
  114.8 19.8 copy-start.22
  117.7 17.9 copy-start.21
  117.7 18.9 copy-start.20
  121.5 17.2 copy-start.18
  121.5 26.6 %collective-permute-start = (bf16[1,13,16,2,768]{4,3,2,1,0:T(2,128)(2,1)}, bf16[1,13,16,2,768]{4,3,2,1,0:T(2,128)(2,1)}, u32[]{:S(2)}, u32[]{:S(2)}) collective-permute-start(bf16[1,13,16,2,768]{4,3,2,1,0:T(2,128)(2,1)} %get-tuple-element.511), channel_id=1, source_target_pairs={{0,4},{1,5},{2,6},{3,7},{8,12},{9,13},{10,14},{11,15},{16,20},{17,... | collective-permute-start | bytes 1916936 | tf_op jit(solution)/shard_map/ppermute | solution.py:19
  126.8 21.3 collective-permute-start.1
  159.6 129.2 %collective-permute-start.2 = (bf16[1,58,13,2,768]{4,3,2,1,0:T(2,128)(2,1)}, bf16[1,58,13,2,768]{4,3,2,1,0:T(2,128)(2,1)}, u32[]{:S(2)}, u32[]{:S(2)}) collective-permute-start(bf16[1,58,13,2,768]{4,3,2,1,0:T(2,128)(2,1)} %get-tuple-element.515), channel_id=1, source_target_pairs={{0,1},{1,2},{2,3},{4,5},{5,6},{6,7},{8,9},{9,10},{10,11},{12,13},{... | collective-permute-start | bytes 6948872 | tf_op jit(solution)/shard_map/ppermute | solution.py:19
  164.6 126.3 %collective-permute-start.3 = (bf16[1,58,13,2,768]{4,3,2,1,0:T(2,128)(2,1)}, bf16[1,58,13,2,768]{4,3,2,1,0:T(2,128)(2,1)}, u32[]{:S(2)}, u32[]{:S(2)}) collective-permute-start(bf16[1,58,13,2,768]{4,3,2,1,0:T(2,128)(2,1)} %get-tuple-element.516), channel_id=1, source_target_pairs={{1,0},{2,1},{3,2},{5,4},{6,5},{7,6},{9,8},{10,9},{11,10},{13,12},{... | collective-permute-start | bytes 6948872 | tf_op jit(solution)/shard_map/ppermute | solution.py:19
  177.6 23.9 %copy-start.27 = (bf16[14,14,768]{2,1,0:T(8,128)(2,1)S(1)}, bf16[14,14,768]{2,1,0:T(8,128)(2,1)}, u32[]{:S(2)}) copy-start(bf16[14,14,768]{2,1,0:T(8,128)(2,1)} %get-tuple-element.542) | copy-start | bytes 903172
  790.4 155.4 %copy-start.42 = (f32[12,12,196]{2,1,0:T(8,128)}, f32[12,12,196]{2,1,0:T(8,128)S(1)}, u32[]{:S(2)}) copy-start(f32[12,12,196]{2,1,0:T(8,128)S(1)} %sub.153) | copy-start | bytes 338692
  790.9 155.0 %copy-start.44 = (f32[12,12,196]{2,1,0:T(8,128)}, f32[12,12,196]{2,1,0:T(8,128)S(1)}, u32[]{:S(2)}) copy-start(f32[12,12,196]{2,1,0:T(8,128)S(1)} %div.89) | copy-start | bytes 338692
  1063.8 20.5 copy-start.5
  1063.8 20.5 copy-start.82
  1086.5 45.1 %copy-start.69 = (f32[512]{0:T(512)}, f32[512]{0:T(512)S(1)}, u32[]{:S(2)}) copy-start(f32[512]{0:T(512)S(1)} %broadcast_multiply_fusion.3) | copy-start | bytes 6148
  1087.6 43.9 %copy-start.78 = (f32[512]{0:T(512)}, f32[512]{0:T(512)S(1)}, u32[]{:S(2)}) copy-start(f32[512]{0:T(512)S(1)} %fusion.176) | copy-start | bytes 6148
  1087.6 20.3 copy-start.10
  1087.7 40.3 %slice-start = ((s8[4718592]{0:T(1024)(128)(4,1)}), s8[524288]{0:T(1024)(128)(4,1)S(1)}, s32[]{:S(2)}) async-start(s8[4718592]{0:T(1024)(128)(4,1)} %bitcast.538), calls=%async_computation.22 | async-start | bytes 1048576
  1107.9 20.1 copy-start.13
  1107.9 20.1 slice-start.1
  1139.5 1013.3 %reduce-scatter.42.cloned.1.call-start = ((), (), s32[]{:S(2)}) async-start(), calls=%async_computation.21 | async-start | bytes 221184
  1175.6 17.1 copy-start.54
  1175.6 17.1 copy-start.57
  1176.1 16.5 copy-start.43
  1192.7 27.1 %copy-start.16 = (f32[12,12,196]{2,1,0:T(8,128)}, f32[12,12,196]{2,1,0:T(8,128)S(1)}, u32[]{:S(2)}) copy-start(f32[12,12,196]{2,1,0:T(8,128)S(1)} %log_add_fusion) | copy-start | bytes 338692
  1192.7 960.9 %reduce-scatter.28.cloned.1.call-start = ((), (), s32[]{:S(2)}) async-start(), calls=%async_computation.14 | async-start | bytes 184320 | tf_op jit(solution)/shard_map/reduce_scatter | solution.py:477
  1375.0 786.1 %reduce-scatter.32.cloned.1.call-start = ((), (), s32[]{:S(2)}) async-start(), calls=%async_computation.16 | async-start | bytes 5308416 | tf_op jit(solution)/shard_map/reduce_scatter | solution.py:454
  1381.7 828.8 %reduce-scatter.40.cloned.1.call-start = ((), (), s32[]{:S(2)}) async-start(), calls=%async_computation.20 | async-start | bytes 5308416
  1560.3 16.5 copy-start.55
  1560.3 16.5 copy-start.58
  1701.4 17.0 copy-start.49
  1701.4 523.6 %reduce-scatter.36.cloned.1.call-start = ((), (), s32[]{:S(2)}) async-start(), calls=%async_computation.18 | async-start | bytes 3981312
  1901.9 85.1 %collective-permute-start.4 = (bf16[1,58,13,2,768]{4,3,2,1,0:T(2,128)(2,1)S(1)}, bf16[1,58,13,2,768]{4,3,2,1,0:T(2,128)(2,1)}, u32[]{:S(2)}, u32[]{:S(2)}) collective-permute-start(bf16[1,58,13,2,768]{4,3,2,1,0:T(2,128)(2,1)S(1)} %copy.226), channel_id=1, source_target_pairs={{1,0},{2,1},{3,2},{5,4},{6,5},{7,6},{9,8},{10,9},{11,10},{13,12},{... | collective-permute-start | bytes 6948872 | tf_op jit(solution)/shard_map/ppermute | solution.py:19
  1907.0 82.0 %collective-permute-start.5 = (bf16[1,58,13,2,768]{4,3,2,1,0:T(2,128)(2,1)}, bf16[1,58,13,2,768]{4,3,2,1,0:T(2,128)(2,1)}, u32[]{:S(2)}, u32[]{:S(2)}) collective-permute-start(bf16[1,58,13,2,768]{4,3,2,1,0:T(2,128)(2,1)} %copy.228), channel_id=1, source_target_pairs={{0,1},{1,2},{2,3},{4,5},{5,6},{6,7},{8,9},{9,10},{10,11},{12,13},{... | collective-permute-start | bytes 6948872 | tf_op jit(solution)/shard_map/ppermute | solution.py:19
  1997.4 22.9 %collective-permute-start.6 = (bf16[1,13,16,2,768]{4,2,1,3,0:T(8,128)(2,1)S(1)}, bf16[1,13,16,2,768]{4,2,1,3,0:T(8,128)(2,1)S(1)}, u32[]{:S(2)}, u32[]{:S(2)}) collective-permute-start(bf16[1,13,16,2,768]{4,2,1,3,0:T(8,128)(2,1)S(1)} %get-tuple-element.513), channel_id=1, source_target_pairs={{4,0},{5,1},{6,2},{7,3},{12,8},{13,9},{14,10},{15,11},{20,16},{21,... | collective-permute-start | bytes 1916936 | tf_op jit(solution)/shard_map/ppermute | solution.py:19
  1998.7 21.6 collective-permute-start.7
  2031.5 195.7 %reduce-scatter.34.cloned.1.call-start = ((), (), s32[]{:S(2)}) async-start(), calls=%async_computation.17 | async-start | bytes 737280 | tf_op jit(solution)/shard_map/reduce_scatter | solution.py:495
  2033.6 23.6 %copy-start.77 = (bf16[768]{0:T(1024)(128)(2,1)S(1)}, bf16[768]{0:T(1024)(128)(2,1)}, u32[]{:S(2)}) copy-start(bf16[768]{0:T(1024)(128)(2,1)} %get-tuple-element.475) | copy-start | bytes 4612
  2033.6 23.7 %copy-start.85 = (bf16[768]{0:T(1024)(128)(2,1)S(1)}, bf16[768]{0:T(1024)(128)(2,1)}, u32[]{:S(2)}) copy-start(bf16[768]{0:T(1024)(128)(2,1)} %get-tuple-element.437) | copy-start | bytes 4612
  2033.7 23.7 %copy-start.84 = (bf16[768]{0:T(1024)(128)(2,1)S(1)}, bf16[768]{0:T(1024)(128)(2,1)}, u32[]{:S(2)}) copy-start(bf16[768]{0:T(1024)(128)(2,1)} %get-tuple-element.441) | copy-start | bytes 4612
  2057.5 21.0 copy-start.50
  2078.8 64.4 %copy-start.15 = (f32[512,768]{1,0:T(8,128)S(1)}, f32[512,768]{1,0:T(8,128)}, u32[]{:S(2)}) copy-start(f32[512,768]{1,0:T(8,128)} %copy-done.12) | copy-start | bytes 4718596
  2078.8 64.4 %copy-start.76 = (f32[3072]{0:T(1024)S(1)}, f32[3072]{0:T(1024)}, u32[]{:S(2)}) copy-start(f32[3072]{0:T(1024)} %convert_element_type.296) | copy-start | bytes 36868
  2155.1 66.9 %copy-start.68 = (f32[512]{0:T(512)S(1)}, f32[512]{0:T(512)}, u32[]{:S(2)}) copy-start(f32[512]{0:T(512)} %copy-done.67) | copy-start | bytes 6148
  2161.1 60.9 %copy-start.8 = (f32[512,768]{1,0:T(8,128)S(1)}, f32[512,768]{1,0:T(8,128)}, u32[]{:S(2)}) copy-start(f32[512,768]{1,0:T(8,128)} %copy-done.7) | copy-start | bytes 4718596
  2161.1 73.3 %reduce-scatter.30.cloned.1.call-start = ((), (), s32[]{:S(2)}) async-start(), calls=%async_computation.15 | async-start | bytes 737280 | tf_op jit(solution)/shard_map/reduce_scatter | solution.py:489
  2161.2 98.4 %copy-start.1 = (bf16[27,64]{1,0:T(8,128)(2,1)S(1)}, bf16[27,64]{1,0:T(8,128)(2,1)}, u32[]{:S(2)}) copy-start(bf16[27,64]{1,0:T(8,128)(2,1)} %param.31) | copy-start | bytes 10372
  2214.9 43.1 %reduce-scatter.26.cloned.1.call-start = ((), (), s32[]{:S(2)}) async-start(), calls=%async_computation.13 | async-start | bytes 552960 | tf_op jit(solution)/shard_map/reduce_scatter | solution.py:468
  (48 other events, 412.2 us)
Sparse Core Ops, SparseCore 0:
  10.8 63.5 all-gather.4
  77.3 52.9 all-gather.6
  133.0 69.8 all-gather.8
  205.6 67.8 all-gather.10
  1139.6 66.3 reduce-scatter.37
  1209.7 59.9 reduce-scatter.41
  1375.1 21.9 reduce-scatter.27
  1400.8 95.2 reduce-scatter.31
  1701.5 98.3 reduce-scatter.39
  2031.6 76.9 reduce-scatter.35
  2161.2 21.8 reduce-scatter.33
  2215.0 19.3 reduce-scatter.29
  2236.9 21.0 reduce-scatter.25
where the time goes:
time: 2290 us; the launch traced here: 2270 us
  local copies, waits for them, and re-layouts  1300 us (57%)
  matrix products  384 us (17%)
  other arithmetic  378 us (17%)
  blocking collectives  126 us (6%)
  waiting for transfers between devices  30.3 us (1%)
  starting transfers between devices  30.2 us (1%)
    reshape x2, local copies, waits for them, and re-layouts, slot_scores(): scores = scores.reshape(slot_count, HEADS, WIN * WIN, WIN * WIN)  349 us
    dynamic_update_slice x36, local copies, waits for them, and re-layouts, place_blocks(): lax.dynamic_update_slice(canvas, current + blocks[slot_index], starts)  213 us
    reshape x1, local copies, waits for them, and re-layouts, attend_back(): d_scores.astype(jnp.float32).reshape(slot_count, HEADS, WIN, WIN, WIN, WIN)  124 us
    reduce_sum x1, other arithmetic, attend_back(): rows_sum = jnp.sum(grid_scores, axis=5)  102 us
    unnamed x276, local copies, waits for them, and re-layouts  99.6 us
    dot_general x1, matrix products, slot_scores(): jnp.einsum('sxyhc,sabhc->shxyab', q_heads, k_heads, preferred_element_typ...  99.1 us
    unnamed x3, blocking collectives  86.3 us
    reduce_sum x1, other arithmetic, attend_core(): denominator = jnp.sum(exponent, axis=-1, keepdims=True)  81.8 us
  transfers between devices with their start and end apart: 21, of which 2 were waited for; matrix products, arithmetic and copies ran while one was open for 89% of the time, Pallas kernels for 0%

commit v1 on v0

v1 whole, which is shorter than its diff:
```python
import functools

import jax
import jax.numpy as jnp
import numpy as np
from jax import lax
from jax.experimental import pallas as pl
from jax.experimental.pallas import tpu as pltpu
from jax.sharding import PartitionSpec as P

D = 768
HEADS = 12
HEAD_DIM = 64
PAIRS = HEADS // 2
WIN = 14
CELLS = WIN * WIN
SLOT = 208
MESH = pl.DeviceIdType.MESH
F32 = jnp.float32
BF16 = jnp.bfloat16
VMEM_LIMIT = 60 * 2**20


def round_up(value, unit):
    return -(-value // unit) * unit


def plan_windows(rows, cols, tile_rows, tile_cols):
    devices = rows * cols
    height, width = rows * tile_rows, cols * tile_cols
    windows = []
    for top in range(0, height, WIN):
        for left in range(0, width, WIN):
            windows.append(
                [
                    (r, c, r - top, c - left)
                    for r in range(top, min(top + WIN, height))
                    for c in range(left, min(left + WIN, width))
                ]
            )
    bins = []
    for window in sorted(windows, key=len, reverse=True):
        for held in bins:
            if len(held) < 2 and sum(map(len, held)) + len(window) <= CELLS:
                held.append(window)
                break
        else:
            bins.append([window])
    slots = -(-len(bins) // devices)
    while len(bins) < slots * devices:
        bins.append([])

    def home(cell):
        return cell[0] // tile_rows * cols + cell[1] // tile_cols

    weights = np.zeros((len(bins), devices), np.int64)
    for number, held in enumerate(bins):
        for window in held:
            for cell in window:
                weights[number, home(cell)] += 1
    hops = np.zeros((devices, devices, rows * rows * cols + cols * cols * rows))
    for source in range(devices):
        for target in range(devices):
            r0, c0, r1, c1 = source // cols, source % cols, target // cols, target % cols
            step = 1 if r1 > r0 else -1
            for r in range(r0, r1, step):
                hops[source, target, (r * rows + r + step) * cols + c0] = 1
            step = 1 if c1 > c0 else -1
            for c in range(c0, c1, step):
                hops[source, target, rows * rows * cols + (c * cols + c + step) * rows + r1] = 1
    loads = np.einsum("bs,sdl->bdl", weights, hops)

    def cost(order):
        load = loads[np.arange(len(bins)), np.array(order) // slots].sum(axis=0)
        return load.max() * 100 + load.sum()

    order = [0] * len(bins)
    free = [slots] * devices
    for number in range(len(bins)):
        options = [d for d in range(devices) if free[d]]
        best = min(options, key=lambda d: (loads[number, d].sum(), d))
        order[number] = best * slots + slots - free[best]
        free[best] -= 1
    current = cost(order)
    while True:
        found = None
        for a in range(len(bins)):
            for b in range(a):
                if order[a] // slots != order[b] // slots:
                    order[a], order[b] = order[b], order[a]
                    trial = cost(order)
                    if trial < current:
                        current, found = trial, (a, b)
                    order[a], order[b] = order[b], order[a]
        if found is None:
            break
        a, b = found
        order[a], order[b] = order[b], order[a]
    total = slots * SLOT
    place = [[] for _ in range(devices)]
    for number in sorted(range(len(bins)), key=lambda n: order[n]):
        device, slot = order[number] // slots, order[number] % slots
        position = slot * SLOT
        for group, window in enumerate(bins[number]):
            for cell in window:
                place[device].append((position, cell, group))
                position += 1
    cells = tile_rows * tile_cols
    pairs = []
    sent, got = [0] * devices, [0] * devices
    moved = {}
    for source in range(devices):
        for target in range(devices):
            if source != target:
                listed = [e for e in place[target] if home(e[1]) == source]
                if listed:
                    count = round_up(len(listed), 16)
                    pairs.append((source, target, sent[source], got[target], count))
                    moved[source, target] = (listed, sent[source], got[target])
                    sent[source] += count
                    got[target] += count
    packed, landed = round_up(max(sent), 128), round_up(max(got), 128)
    pack_from = np.full((devices, packed), -1, np.int32)
    slot_from = np.full((devices, total), -1, np.int32)
    back_from = np.full((devices, landed), -1, np.int32)
    tile_from = np.full((devices, cells), -1, np.int32)
    where = np.full((devices, total, 8), -1, np.int32)
    for device in range(devices):
        for position, cell, group in place[device]:
            where[device, position, :5] = (cell[2], cell[3], group, cell[0], cell[1])
            if home(cell) == device:
                local = cell[0] % tile_rows * tile_cols + cell[1] % tile_cols
                slot_from[device, position] = local
                tile_from[device, local] = position
    for (source, target), (listed, out, into) in moved.items():
        for k, (position, cell, group) in enumerate(listed):
            local = cell[0] % tile_rows * tile_cols + cell[1] % tile_cols
            pack_from[source, out + k] = local
            slot_from[target, position] = cells + into + k
            back_from[target, into + k] = position
            tile_from[source, local] = total + out + k
    return dict(
        slots=slots, total=total, pairs=pairs, packed=packed, landed=landed, where=where,
        pack_from=pack_from, slot_from=slot_from, back_from=back_from, tile_from=tile_from,
    )


def matmul(a, b):
    return jnp.dot(a, b, preferred_element_type=F32)


def matmul_nt(a, b):
    return lax.dot_general(a, b, (((1,), (1,)), ((), ())), preferred_element_type=F32)


def matmul_tn(a, b):
    return lax.dot_general(a, b, (((0,), (0,)), ((), ())), preferred_element_type=F32)


def one_hot(index, width):
    return (index == lax.broadcasted_iota(jnp.int32, (index.shape[0], width), 1)).astype(BF16)


def normalized(values):
    offset = values - jnp.mean(values, axis=-1, keepdims=True)
    rate = lax.rsqrt(jnp.mean(offset * offset, axis=-1, keepdims=True) + 1e-06)
    return offset * rate, rate


def norm_back(cotangent, gain, hat, rate):
    e = cotangent * gain
    mean_e = jnp.mean(e, axis=-1, keepdims=True)
    mean_eh = jnp.mean(e * hat, axis=-1, keepdims=True)
    return rate * (e - mean_e - hat * mean_eh)


def column_sum(values):
    return jnp.sum(values, axis=0, keepdims=True)


def whole(shape):
    return pl.BlockSpec(shape, lambda *_: (0,) * len(shape))


def params(**more):
    return pltpu.CompilerParams(vmem_limit_bytes=VMEM_LIMIT, **more)


def qkv_kernel(x_ref, vec_ref, mask_ref, where_ref, w_ref, n1_ref, qkv_ref, key_ref):
    hat, _ = normalized(x_ref[...].astype(F32))
    n1_ref[...] = (hat * vec_ref[0:1, :] + vec_ref[1:2, :]).astype(BF16)
    for part in range(3):
        columns = pl.ds(part * D, D)
        out = matmul(n1_ref[...], w_ref[:, columns])
        if part == 0:
            out = out + vec_ref[2:3, :]
        if part == 2:
            out = out + vec_ref[3:4, :]
        qkv_ref[:, columns] = out.astype(BF16)
    place = where_ref[...]
    rows = matmul(one_hot(place[:, 3:4], mask_ref.shape[0]), mask_ref[...])
    lane = lax.broadcasted_iota(jnp.int32, rows.shape, 1)
    valid = jnp.sum(jnp.where(lane == place[:, 4:5], rows, 0.0), axis=1, keepdims=True)
    lane = lax.broadcasted_iota(jnp.int32, key_ref.shape, 1)
    hot = (lane == place[:, 0:1]) | ((lane == place[:, 1:2] + WIN) & (place[:, 1:2] >= 0))
    group = lane - 2 * WIN
    shut = ((group == 0) | (group == 1)) & ((valid < 0.5) | (place[:, 2:3] != group))
    key_ref[...] = jnp.where(shut, -1e30, jnp.where(hot, 1.0, 0.0)).astype(BF16)


def head_halves(pair):
    low = lax.broadcasted_iota(jnp.int32, pair.shape, 1) < HEAD_DIM
    zero = jnp.zeros_like(pair)
    return jnp.concatenate([jnp.where(low, pair, zero), jnp.where(low, zero, pair)], axis=0)


def join_halves(stacked):
    low = lax.broadcasted_iota(jnp.int32, (SLOT, 2 * HEAD_DIM), 1) < HEAD_DIM
    return jnp.where(low, stacked[:SLOT], stacked[SLOT:])


REL = 512


def own_place(where_ref):
    lane = lax.broadcasted_iota(jnp.int32, (SLOT, REL), 1)
    row, col = where_ref[:, 0:1], where_ref[:, 1:2]
    first, second = row * WIN, REL // 2 + col * WIN
    hot = (lane >= first) & (lane < first + WIN) & (row >= 0)
    hot = hot | ((lane >= second) & (lane < second + WIN) & (col >= 0))
    return jnp.where(hot, 1.0, 0.0).astype(BF16)


def attend_kernel(q_ref, k_ref, v_ref, key_ref, where_ref, rel_ref, fold_ref, o_ref, p_ref, own_ref):
    @pl.when(pl.program_id(1) == 0)
    def _():
        own_ref[...] = own_place(where_ref)

    qs = head_halves(q_ref[...])
    own = own_ref[...]
    own2 = jnp.concatenate([own, own], axis=0)
    spread = matmul(qs, rel_ref[...]).astype(BF16) * own2
    lane = lax.broadcasted_iota(jnp.int32, (SLOT, 128), 1)
    group = lane - 2 * WIN
    second = where_ref[:, 2:3] == 1
    mark = jnp.where(((group == 0) & ~second) | ((group == 1) & second), 1.0, 0.0)
    near = matmul(spread, fold_ref[...]) + jnp.concatenate([mark, mark], axis=0)
    left = jnp.concatenate([qs * BF16(0.125), near.astype(BF16)], axis=1)
    right = jnp.concatenate([k_ref[...], key_ref[...]], axis=1)
    scores = matmul_nt(left, right)
    weight = jnp.exp(scores - jnp.max(scores, axis=-1, keepdims=True))
    soft = (weight / jnp.sum(weight, axis=-1, keepdims=True)).astype(BF16)
    p_ref[...] = soft
    o_ref[...] = join_halves(matmul(soft, v_ref[...])).astype(BF16)


def attend_back_kernel(
    q_ref, k_ref, v_ref, o_ref, do_ref, p_ref, key_ref, where_ref, rel_ref, fold_ref,
    dq_ref, dk_ref, dv_ref, drel_ref, own_ref,
):
    @pl.when(pl.program_id(1) == 0)
    def _():
        own_ref[...] = own_place(where_ref)

    @pl.when((pl.program_id(0) == 0) & (pl.program_id(1) == 0))
    def _():
        drel_ref[...] = jnp.zeros_like(drel_ref)

    qs, dos = head_halves(q_ref[...]), head_halves(do_ref[...])
    o = o_ref[...].astype(F32)
    soft = p_ref[...]
    inner = jnp.sum(dos.astype(F32) * jnp.concatenate([o, o], axis=0), axis=-1, keepdims=True)
    ds = (soft.astype(F32) * (matmul_nt(dos, v_ref[...]) - inner)).astype(BF16)
    right = jnp.concatenate([k_ref[...], key_ref[...]], axis=1)
    back = matmul(ds, right)
    own = own_ref[...]
    own2 = jnp.concatenate([own, own], axis=0)
    spread = matmul_nt(back[:, 128:].astype(BF16), fold_ref[...]).astype(BF16) * own2
    dq = back[:, :128] * 0.125 + matmul_nt(spread, rel_ref[...])
    dq_ref[...] = join_halves(dq).astype(BF16)
    drel_ref[...] += matmul_tn(qs, spread)
    dk_ref[...] = (matmul_tn(ds, qs) * 0.125).astype(BF16)
    dv_ref[...] = matmul_tn(soft, dos).astype(BF16)


def rel_tables(rel_rows, rel_cols):
    index = np.arange(WIN)[:, None] - np.arange(WIN)[None, :] + WIN - 1
    select = np.zeros((2, 2 * WIN - 1, REL // 2), np.float32)
    select[:, index.reshape(-1), np.arange(CELLS)] = 1
    rel = jnp.concatenate(
        [
            jnp.einsum("mc,ml->cl", table, select[0].astype(BF16), preferred_element_type=F32)
            for table in (rel_rows, rel_cols)
        ],
        axis=1,
    ).astype(BF16)
    fold = np.zeros((REL, 128), np.float32)
    for first in range(WIN):
        for second in range(WIN):
            fold[first * WIN + second, second] = 1
            fold[REL // 2 + first * WIN + second, WIN + second] = 1
    return jnp.concatenate([rel, rel], axis=0), jnp.asarray(fold, BF16), select[0]


def proj_kernel(o_ref, x_ref, vec_ref, w_ref, r_ref, n2_ref):
    r = x_ref[...].astype(F32) + matmul(o_ref[...], w_ref[...]) + vec_ref[4:5, :]
    r_ref[...] = r
    hat, _ = normalized(r)
    n2_ref[...] = (hat * vec_ref[5:6, :] + vec_ref[6:7, :]).astype(BF16)


def mlp_kernel(n2_ref, g_ref, r_ref, vec_ref, b1_ref, w1_ref, w2_ref, out_ref, dn2_ref, dw1_ref, dw2_ref, db1_ref, acc_ref):
    step = pl.program_id(0)

    @pl.when(step == 0)
    def _():
        acc_ref[...] = r_ref[...] + vec_ref[7:8, :]
        dn2_ref[...] = jnp.zeros_like(dn2_ref)

    n2, g = n2_ref[...], g_ref[...]
    w1, w2 = w1_ref[...], w2_ref[...]
    u = matmul(n2, w1) + b1_ref[...]
    half = 0.5 + 0.5 * lax.erf(u * 0.7071067811865476)
    slope = half + u * jnp.exp(u * u * -0.5) * 0.3989422804014327
    a = (u * half).astype(BF16)
    acc_ref[...] += matmul(a, w2)
    dw2_ref[...] = matmul_tn(a, g).astype(BF16)
    du = matmul_nt(g, w2) * slope
    du = du.astype(BF16)
    db1_ref[...] = column_sum(du.astype(F32))
    dw1_ref[...] = matmul_tn(n2, du).astype(BF16)
    dn2_ref[...] += matmul_nt(du, w1)

    @pl.when(step == pl.num_programs(0) - 1)
    def _():
        out_ref[...] = acc_ref[...].astype(BF16)


def proj_back_kernel(dn2_ref, r_ref, g_ref, o_ref, vec_ref, w_ref, dr_ref, do_ref, dw_ref, sums_ref):
    hat, rate = normalized(r_ref[...])
    dn2, g = dn2_ref[...], g_ref[...].astype(F32)
    sums_ref[0:1, :] = column_sum(dn2 * hat)
    sums_ref[1:2, :] = column_sum(dn2)
    sums_ref[2:3, :] = column_sum(g)
    dr = g + norm_back(dn2, vec_ref[5:6, :], hat, rate)
    dr_ref[...] = dr
    db = dr.astype(BF16)
    sums_ref[3:4, :] = column_sum(db.astype(F32))
    dw_ref[...] = matmul_tn(o_ref[...], db).astype(BF16)
    do_ref[...] = matmul_nt(db, w_ref[...]).astype(BF16)


def qkv_back_kernel(dq_ref, dk_ref, dv_ref, n1_ref, x_ref, dr_ref, vec_ref, w_ref, gx_ref, dw_ref, sums_ref):
    hat, rate = normalized(x_ref[...].astype(F32))
    dn1 = None
    for part, ref in enumerate((dq_ref, dk_ref, dv_ref)):
        columns = pl.ds(part * D, D)
        term = matmul_nt(ref[...], w_ref[:, columns])
        dn1 = term if dn1 is None else dn1 + term
        dw_ref[:, columns] = matmul_tn(n1_ref[...], ref[...]).astype(BF16)
    sums_ref[0:1, :] = column_sum(dn1 * hat)
    sums_ref[1:2, :] = column_sum(dn1)
    sums_ref[2:3, :] = column_sum(dq_ref[...].astype(F32))
    sums_ref[3:4, :] = column_sum(dv_ref[...].astype(F32))
    gx_ref[...] = (dr_ref[...] + norm_back(dn1, vec_ref[0:1, :], hat, rate)).astype(BF16)


def call(kernel, out_shapes, *operands, **more):
    return pl.pallas_call(
        kernel,
        out_shape=[jax.ShapeDtypeStruct(shape, kind) for shape, kind in out_shapes],
        compiler_params=params(),
        **more,
    )(*operands)


def compute(plan, xs, gs, mask, where, rel_rows, rel_cols, vec, b1, w_qkv, w_proj, w_fc1, w_fc2):
    total, slots = plan["total"], plan["slots"]
    ff = w_fc1.shape[1]
    rel, fold, select = rel_tables(rel_rows, rel_cols)
    n1, qkv, key = call(
        qkv_kernel,
        [((total, D), BF16), ((total, 3 * D), BF16), ((total, 128), BF16)],
        xs, vec, mask, where, w_qkv,
    )

    def slab(offset):
        return pl.BlockSpec((SLOT, 128), lambda s, p: (s, offset + p))

    per_slot = pl.BlockSpec((SLOT, 128), lambda s, p: (s, 0))
    place = pl.BlockSpec((SLOT, 8), lambda s, p: (s, 0))
    soft_spec = pl.BlockSpec((None, None, 2 * SLOT, SLOT), lambda s, p: (s, p, 0, 0))
    o, soft = call(
        attend_kernel,
        [((total, D), BF16), ((slots, PAIRS, 2 * SLOT, SLOT), BF16)],
        qkv, qkv, qkv, key, where, rel, fold,
        grid=(slots, PAIRS),
        in_specs=[slab(0), slab(PAIRS), slab(2 * PAIRS), per_slot, place, whole(rel.shape), whole(fold.shape)],
        out_specs=[slab(0), soft_spec],
        scratch_shapes=[pltpu.VMEM((SLOT, REL), BF16)],
    )
    r, n2 = call(proj_kernel, [((total, D), F32), ((total, D), BF16)], o, xs, vec, w_proj)
    block = 512
    steps = ff // block
    out, dn2, dw_fc1, dw_fc2, db1 = call(
        mlp_kernel,
        [((total, D), BF16), ((total, D), F32), ((D, ff), BF16), ((ff, D), BF16), ((1, ff), F32)],
        n2, gs, r, vec, b1, w_fc1, w_fc2,
        grid=(steps,),
        in_specs=[
            whole((total, D)), whole((total, D)), whole((total, D)), whole(vec.shape),
            pl.BlockSpec((1, block), lambda f: (0, f)),
            pl.BlockSpec((D, block), lambda f: (0, f)),
            pl.BlockSpec((block, D), lambda f: (f, 0)),
        ],
        out_specs=[
            whole((total, D)), whole((total, D)),
            pl.BlockSpec((D, block), lambda f: (0, f)),
            pl.BlockSpec((block, D), lambda f: (f, 0)),
            pl.BlockSpec((1, block), lambda f: (0, f)),
        ],
        scratch_shapes=[pltpu.VMEM((total, D), F32)],
    )
    dr, do, dw_proj, sums2 = call(
        proj_back_kernel,
        [((total, D), F32), ((total, D), BF16), ((D, D), BF16), ((8, D), F32)],
        dn2, r, gs, o, vec, w_proj,
    )
    dq, dk, dv, drel = call(
        attend_back_kernel,
        [((total, D), BF16)] * 3 + [((128, REL), F32)],
        qkv, qkv, qkv, o, do, soft, key, where, rel, fold,
        grid=(slots, PAIRS),
        in_specs=[
            slab(0), slab(PAIRS), slab(2 * PAIRS), slab(0), slab(0), soft_spec,
            per_slot, place, whole(rel.shape), whole(fold.shape),
        ],
        out_specs=[slab(0), slab(0), slab(0), whole((128, REL))],
        scratch_shapes=[pltpu.VMEM((SLOT, REL), BF16)],
    )
    gx, dw_qkv, sums1 = call(
        qkv_back_kernel,
        [((total, D), BF16), ((D, 3 * D), BF16), ((8, D), F32)],
        dq, dk, dv, n1, xs, dr, vec, w_qkv,
    )
    drel = drel[:HEAD_DIM] + drel[HEAD_DIM:]
    half = REL // 2
    drel_rows = jnp.einsum("ml,cl->mc", select, drel[:, :half], precision=lax.Precision.HIGHEST)
    drel_cols = jnp.einsum("ml,cl->mc", select, drel[:, half:], precision=lax.Precision.HIGHEST)
    sums = [sums1[0], sums1[1], sums1[2], sums1[3], sums2[3], sums2[0], sums2[1], sums2[2]]
    return out, gx, dw_qkv, dw_proj, dw_fc1, dw_fc2, jnp.stack(sums), db1, drel_rows, drel_cols


def axis_sizes():
    return lax.axis_size("img"), lax.axis_size("row"), lax.axis_size("col")


class Place:
    def __init__(self):
        images, self.rows, self.cols = axis_sizes()
        self.chips = images // 2
        img = lax.axis_index("img")
        self.chip, self.core = img // 2, img % 2
        self.row, self.col = lax.axis_index("row"), lax.axis_index("col")

    def other(self, axis, k):
        if axis == "row":
            index = (self.row + k) % self.rows
            return index, {"row": index}
        if axis == "col":
            index = (self.col + k) % self.cols
            return index, {"col": index}
        index = (self.chip + k) % self.chips
        return index, {"img": index * 2 + self.core}

    def sibling(self):
        return {"img": self.chip * 2 + 1 - self.core}

    def count(self, axis):
        return {"row": self.rows, "col": self.cols, "chip": self.chips}[axis]


def greet(place, image_wide):
    barrier = pltpu.get_barrier_semaphore()
    heard = 1
    pl.semaphore_signal(barrier, inc=1, device_id=place.sibling(), device_id_type=MESH)
    for k in range(1, place.chips):
        pl.semaphore_signal(barrier, inc=1, device_id=place.other("chip", k)[1], device_id_type=MESH)
        heard += 1
    for r in range(place.rows):
        for c in range(place.cols):
            if (r, c) == (0, 0) or not (image_wide or r == 0 or c == 0):
                continue
            target = {"row": (place.row + r) % place.rows, "col": (place.col + c) % place.cols}
            pl.semaphore_signal(barrier, inc=1, device_id=target, device_id_type=MESH)
            heard += 1
    pl.semaphore_wait(barrier, heard)


class Copies:
    def __init__(self, send_sems, recv_sems):
        self.send_sems, self.recv_sems = send_sems, recv_sems
        self.used = 0
        self.open = []

    def start(self, source, target, device):
        copy = pltpu.make_async_remote_copy(
            src_ref=source,
            dst_ref=target,
            send_sem=self.send_sems.at[self.used],
            recv_sem=self.recv_sems.at[self.used],
            device_id=device,
            device_id_type=MESH,
        )
        self.used += 1
        copy.start()
        self.open.append(copy)
        return copy

    def finish(self):
        for copy in self.open:
            copy.wait_send()
        self.open = []


def gather_copies(rows, cols, chips):
    return (cols - 1) + (rows - 1) + (chips - 1) + rows * (chips - 1) + chips * (rows - 1) + chips


def gather_phase(place, copies, phase, shard, full, local):
    y, c, x, z = place.chip, place.core, place.row, place.col
    half = place.cols // 2
    low, high = pl.ds(0, half), pl.ds(half, place.cols - half)
    started = []
    if phase == 0:
        keep = pltpu.make_async_copy(shard, full.at[y, c, x, z], local)
        keep.start()
        for k in range(1, place.cols):
            started.append(copies.start(shard, full.at[y, c, x, z], place.other("col", k)[1]))
        return started, keep
    if phase == 1:
        for k in range(1, place.rows):
            part = full.at[y, c, x, low]
            started.append(copies.start(part, part, place.other("row", k)[1]))
        for k in range(1, place.chips):
            part = full.at[y, c, x, high]
            started.append(copies.start(part, part, place.other("chip", k)[1]))
    if phase == 2:
        for k in range(1, place.chips):
            for row in range(place.rows):
                part = full.at[y, c, row, low]
                started.append(copies.start(part, part, place.other("chip", k)[1]))
        for k in range(1, place.rows):
            for chip in range(place.chips):
                part = full.at[chip, c, x, high]
                started.append(copies.start(part, part, place.other("row", k)[1]))
    if phase == 3:
        for chip in range(place.chips):
            part = full.at[chip, c]
            started.append(copies.start(part, part, place.sibling()))
    return started, None


def wait_phase(started):
    copies, keep = started
    if keep is not None:
        keep.wait()
    for copy in copies:
        copy.wait_recv()


def gather_kernel(groups, *refs):
    count = sum(map(len, groups))
    shards, fulls = refs[:count], refs[count : 2 * count]
    send_sems, recv_sems, local_sems = refs[2 * count :]
    place = Place()
    greet(place, False)
    copies = Copies(send_sems, recv_sems)
    waiting = {}
    for step in range(len(groups) + 4):
        for number in range(len(groups)):
            phase = step - number
            if 0 <= phase <= 4:
                for item in groups[number]:
                    if phase > 0:
                        wait_phase(waiting.pop(item))
                    if phase < 4:
                        waiting[item] = gather_phase(
                            place, copies, phase, shards[item], fulls[item], local_sems.at[item]
                        )
    copies.finish()


def gather(shards, groups, number):
    images, rows, cols = axis_sizes()
    chips = images // 2
    each = gather_copies(rows, cols, chips)
    anywhere = pl.BlockSpec(memory_space=pl.ANY)
    fulls = pl.pallas_call(
        functools.partial(gather_kernel, groups),
        out_shape=[
            jax.ShapeDtypeStruct((chips, 2, rows, cols) + shard.shape, shard.dtype) for shard in shards
        ],
        in_specs=[anywhere] * len(shards),
        out_specs=[anywhere] * len(shards),
        scratch_shapes=[
            pltpu.SemaphoreType.DMA((each * len(shards),)),
            pltpu.SemaphoreType.DMA((each * len(shards),)),
            pltpu.SemaphoreType.DMA((len(shards),)),
        ],
        compiler_params=params(collective_id=number, has_side_effects=True),
    )(*shards)
    return fulls


def scatter_copies(rows, cols, chips):
    return chips + (chips - 1) + (rows - 1) + (rows - 1) + (chips - 1) + (cols - 1)


def scatter_buffers(shape, rows, cols, chips):
    half = cols // 2
    rest = cols - half
    return [
        pltpu.VMEM((chips, rows, cols) + shape, BF16),
        pltpu.VMEM((chips, rows, cols) + shape, BF16),
        pltpu.VMEM((chips - 1, rows, half) + shape, BF16),
        pltpu.VMEM((rows - 1, chips, rest) + shape, BF16),
        pltpu.VMEM((rows - 1, half) + shape, BF16),
        pltpu.VMEM((chips - 1, rest) + shape, BF16),
        pltpu.VMEM((cols - 1,) + shape, BF16),
    ]


def add_into(target, index, terms):
    total = target[index].astype(F32)
    for ref, at in terms:
        total = total + ref[at].astype(F32)
    target[index] = total.astype(BF16)


def scatter_phase(place, copies, phase, full, out, buffers, local):
    y, c, x, z = place.chip, place.core, place.row, place.col
    mine, twin, low_chip, high_row, low_row, high_chip, along = buffers
    half = place.cols // 2
    rest = place.cols - half
    low, high = pl.ds(0, half), pl.ds(half, rest)
    started, keep = [], None
    if phase == 0:
        keep = pltpu.make_async_copy(full.at[:, c], mine, local)
        keep.start()
        for chip in range(place.chips):
            started.append(copies.start(full.at[chip, 1 - c], twin.at[chip], place.sibling()))
    if phase == 1:

        @pl.loop(0, place.chips * place.rows * place.cols)
        def _(n):
            index = (n // (place.rows * place.cols), n // place.cols % place.rows, n % place.cols)
            add_into(mine, index, [(twin, index)])

        for k in range(1, place.chips):
            to, device = place.other("chip", k)
            started.append(copies.start(mine.at[to, :, low], low_chip.at[k - 1], device))
        for k in range(1, place.rows):
            to, device = place.other("row", k)
            started.append(copies.start(mine.at[:, to, high], high_row.at[k - 1], device))
    if phase == 2:

        @pl.loop(0, place.rows * half)
        def _(n):
            r, j = n // half, n % half
            add_into(mine, (y, r, j), [(low_chip, (k, r, j)) for k in range(place.chips - 1)])

        @pl.loop(0, place.chips * rest)
        def _(n):
            chip, j = n // rest, n % rest
            add_into(mine, (chip, x, half + j), [(high_row, (k, chip, j)) for k in range(place.rows - 1)])

        for k in range(1, place.rows):
            to, device = place.other("row", k)
            started.append(copies.start(mine.at[y, to, low], low_row.at[k - 1], device))
        for k in range(1, place.chips):
            to, device = place.other("chip", k)
            started.append(copies.start(mine.at[to, x, high], high_chip.at[k - 1], device))
    if phase == 3:
        for j in range(half):
            add_into(mine, (y, x, j), [(low_row, (k, j)) for k in range(place.rows - 1)])
        for j in range(rest):
            add_into(mine, (y, x, half + j), [(high_chip, (k, j)) for k in range(place.chips - 1)])
        for k in range(1, place.cols):
            to, device = place.other("col", k)
            started.append(copies.start(mine.at[y, x, to], along.at[k - 1], device))
    if phase == 4:
        total = mine[y, x, z].astype(F32)
        for k in range(place.cols - 1):
            total = total + along[k].astype(F32)
        out[...] = total
    return started, keep


def swap_steps(place):
    steps = [place.sibling()]
    bit = 1
    while bit < place.chips:
        flip = place.chip + bit - 2 * bit * (place.chip // bit % 2)
        steps.append({"img": flip * 2 + place.core})
        bit *= 2
    bit = 1
    while bit < place.rows:
        steps.append({"row": place.row + bit - 2 * bit * (place.row // bit % 2)})
        bit *= 2
    bit = 1
    while bit < place.cols:
        steps.append({"col": place.col + bit - 2 * bit * (place.col // bit % 2)})
        bit *= 2
    return steps


def scatter_kernel(groups, with_sum, *refs):
    count = sum(map(len, groups))
    refs = list(refs)

    def take(n):
        taken = refs[:n]
        del refs[:n]
        return taken

    fulls = take(count)
    term = take(1)[0] if with_sum else None
    outs = take(count)
    total = take(1)[0] if with_sum else None
    buffers = [take(7) for _ in range(count)]
    send_sems, recv_sems, local_sems = take(3)
    place = Place()
    greet(place, False)
    copies = Copies(send_sems, recv_sems)
    waiting = {}
    swaps = swap_steps(place) if with_sum else []
    if with_sum:
        held, arriving = take(2)
        held[0] = term[...]
    swap = None
    for step in range(max(len(groups) + 4, len(swaps) + 1)):
        if swap is not None:
            swap.wait_recv()
            held[step] = held[step - 1] + arriving[step - 1]
            swap = None
            if step == len(swaps):
                total[...] = held[step]
        if step < len(swaps):
            swap = copies.start(held.at[step], arriving.at[step], swaps[step])
        for number in range(len(groups)):
            phase = step - number
            if 0 <= phase <= 4:
                for item in groups[number]:
                    if phase > 0:
                        wait_phase(waiting.pop(item))
                    waiting[item] = scatter_phase(
                        place, copies, phase, fulls[item], outs[item], buffers[item], local_sems.at[item]
                    )
    copies.finish()


def scatter(fulls, groups, number, term=None):
    images, rows, cols = axis_sizes()
    chips = images // 2
    shapes = [full.shape[4:] for full in fulls]
    swaps = (images * rows * cols).bit_length() - 1
    extra = swaps if term is not None else 0
    each = scatter_copies(rows, cols, chips)
    anywhere = pl.BlockSpec(memory_space=pl.ANY)
    vmem = pl.BlockSpec(memory_space=pltpu.VMEM)
    scratch = sum([scatter_buffers(shape, rows, cols, chips) for shape in shapes], [])
    scratch += [
        pltpu.SemaphoreType.DMA((each * len(fulls) + extra,)),
        pltpu.SemaphoreType.DMA((each * len(fulls) + extra,)),
        pltpu.SemaphoreType.DMA((len(fulls),)),
    ]
    out_shape = [jax.ShapeDtypeStruct(shape, F32) for shape in shapes]
    operands = list(fulls)
    in_specs = [anywhere] * len(fulls)
    if term is not None:
        operands.append(term)
        in_specs.append(vmem)
        out_shape.append(jax.ShapeDtypeStruct(term.shape, F32))
        scratch += [pltpu.VMEM((swaps + 1,) + term.shape, F32), pltpu.VMEM((swaps,) + term.shape, F32)]
    return pl.pallas_call(
        functools.partial(scatter_kernel, groups, term is not None),
        out_shape=out_shape,
        in_specs=in_specs,
        out_specs=[vmem] * len(out_shape),
        scratch_shapes=scratch,
        compiler_params=params(collective_id=number, has_side_effects=True),
    )(*operands)


def exchange(place, copies, plan, source, target, back):
    me = place.row * place.cols + place.col
    first = copies.used
    for number, (giver, taker, out, into, count) in enumerate(plan["pairs"]):
        if back:
            giver, taker, out, into = taker, giver, into, out

        def describe(giver=giver, taker=taker, out=out, into=into, count=count, number=number):
            return pltpu.make_async_remote_copy(
                src_ref=source.at[pl.ds(out, count)],
                dst_ref=target.at[pl.ds(into, count)],
                send_sem=copies.send_sems.at[first + number],
                recv_sem=copies.recv_sems.at[first + number],
                device_id={"row": taker // place.cols, "col": taker % place.cols},
                device_id_type=MESH,
            )

        yield me, giver, taker, describe
    copies.used = first + len(plan["pairs"])


def windows_kernel(plan, back, *refs):
    count = len(refs) - 6
    arrays, pack_ref, place_ref = refs[: count // 2], refs[count // 2], refs[count // 2 + 1]
    outs = refs[count // 2 + 2 : count + 2]
    packed, landed, send_sems, recv_sems = refs[count + 2 : count + 6]
    landed[...] = jnp.zeros_like(landed)
    place = Place()
    greet(place, True)
    copies = Copies(send_sems, recv_sems)
    pick = one_hot(pack_ref[...], arrays[0].shape[0])
    for k, array in enumerate(arrays):
        packed[:, pl.ds(k * D, D)] = matmul(pick, array[...]).astype(BF16)
    listed = list(exchange(place, copies, plan, packed, landed, back))
    for me, giver, taker, describe in listed:

        @pl.when(me == giver)
        def _():
            describe().start()

    index = place_ref[...]
    here = one_hot(index, arrays[0].shape[0])
    for k, array in enumerate(arrays):
        outs[k][...] = matmul(here, array[...]).astype(BF16)
    for me, giver, taker, describe in listed:

        @pl.when(me == taker)
        def _():
            describe().wait_recv()

    there = one_hot(index - arrays[0].shape[0], landed.shape[0])
    for k in range(len(arrays)):
        outs[k][...] += matmul(there, landed[:, pl.ds(k * D, D)]).astype(BF16)
    for me, giver, taker, describe in listed:

        @pl.when(me == giver)
        def _():
            describe().wait_send()


def move_windows(plan, arrays, pick, index, back, number):
    length = index.shape[0]
    landed = plan["packed"] if back else plan["landed"]
    vmem = pl.BlockSpec(memory_space=pltpu.VMEM)

    def kernel(*refs):
        windows_kernel(plan, back, *refs)

    return pl.pallas_call(
        kernel,
        out_shape=[jax.ShapeDtypeStruct((length, D), BF16) for _ in arrays],
        in_specs=[vmem] * (len(arrays) + 2),
        out_specs=[vmem] * len(arrays),
        scratch_shapes=[
            pltpu.VMEM((pick.shape[0], len(arrays) * D), BF16),
            pltpu.VMEM((landed, len(arrays) * D), BF16),
            pltpu.SemaphoreType.DMA((len(plan["pairs"]),)),
            pltpu.SemaphoreType.DMA((len(plan["pairs"]),)),
        ],
        compiler_params=params(collective_id=number, has_side_effects=True),
    )(*arrays, pick, index)


def slab_shape(shape):
    return shape if shape[0] % 8 == 0 else (shape[0] * shape[1] // 128, 128)


def body(
    image_tokens, cotangent, content_mask, norm1_gain, norm1_bias, qkv_weight, query_bias, value_bias,
    rel_rows, rel_cols, proj_weight, proj_bias, norm2_gain, norm2_bias, fc1_weight, fc1_bias, fc2_weight, fc2_bias,
):
    images, rows, cols = axis_sizes()
    chips, devices = images // 2, images * rows * cols
    _, tile_rows, tile_cols, _ = image_tokens.shape
    plan = plan_windows(rows, cols, tile_rows, tile_cols)
    me = lax.axis_index("row") * cols + lax.axis_index("col")

    def own(table):
        return lax.dynamic_index_in_dim(jnp.asarray(table), me, keepdims=False)

    pick, slot_index = own(plan["pack_from"])[:, None], own(plan["slot_from"])[:, None]
    back_pick, tile_index = own(plan["back_from"])[:, None], own(plan["tile_from"])[:, None]
    where = own(plan["where"])

    vectors = [norm1_gain, norm1_bias, query_bias, value_bias, proj_bias, norm2_gain, norm2_bias, fc2_bias]
    piece, wide = norm1_gain.shape[0], fc1_bias.shape[0]
    flat = jnp.concatenate(vectors + [fc1_bias])
    used = flat.shape[0]
    padded = round_up(used, 2048)
    small = jnp.pad(flat, (0, padded - used)).reshape(padded // 128, 128)
    weights = [qkv_weight, proj_weight, fc1_weight, fc2_weight]
    shards = [small] + [w.reshape(slab_shape(w.shape)) for w in weights]

    tokens, grads = (a.reshape(tile_rows * tile_cols, D) for a in (image_tokens, cotangent))
    xs, gs = move_windows(plan, [tokens, grads], pick, slot_index, False, 0)
    fulls = gather(shards, [[0, 1], [2, 3], [4]], 1)
    lists = fulls[0].reshape(devices, padded)[:, :used].astype(F32)
    vec = lists[:, : 8 * piece].reshape(devices, 8, piece).transpose(1, 0, 2).reshape(8, devices * piece)
    b1 = lists[:, 8 * piece :].reshape(1, devices * wide)
    whole_weights = [
        full.reshape((devices * w.shape[0],) + w.shape[1:]) for full, w in zip(fulls[1:], weights)
    ]
    out, gx, dw_qkv, dw_proj, dw_fc1, dw_fc2, sums, db1, drel_rows, drel_cols = compute(
        plan, xs, gs, content_mask[0].astype(BF16), where, rel_rows, rel_cols, vec, b1, *whole_weights
    )
    split = jnp.concatenate(
        [sums.reshape(8, devices, piece).transpose(1, 0, 2).reshape(devices, 8 * piece), db1.reshape(devices, wide)],
        axis=1,
    ).astype(BF16)
    split = jnp.pad(split, ((0, 0), (0, padded - used))).reshape((devices,) + small.shape)
    term = jnp.concatenate([drel_rows, drel_cols], axis=1)
    term = jnp.pad(term, ((0, 32 - term.shape[0]), (0, 0)))
    partial = [split, dw_qkv, dw_proj, dw_fc1, dw_fc2]
    partial = [p.reshape((chips, 2, rows, cols) + s.shape) for p, s in zip(partial, shards)]
    *parts, rel_total = scatter(partial, [[3, 4], [2], [1, 0]], 2, term)
    out, gx = move_windows(plan, [out, gx], back_pick, tile_index, True, 3)
    flat = parts[0].reshape(padded)
    g_vec = [flat[k * piece : (k + 1) * piece] for k in range(8)]
    g_b1 = flat[8 * piece : 8 * piece + wide]
    g_qkv, g_proj, g_fc1, g_fc2 = (p.reshape(w.shape) for p, w in zip(parts[1:], weights))
    span = rel_rows.shape[0]
    return (
        out.reshape(image_tokens.shape), gx.reshape(image_tokens.shape),
        g_vec[0], g_vec[1], g_qkv, g_vec[2], g_vec[3],
        rel_total[:span, :HEAD_DIM], rel_total[:span, HEAD_DIM:],
        g_proj, g_vec[4], g_vec[5], g_vec[6], g_fc1, g_b1, g_fc2, g_vec[7],
    )


def solution(mesh):
    everywhere = ("img", "row", "col")
    tile, vector, matrix = P("img", "row", "col", None), P(everywhere), P(everywhere, None)
    in_specs = (
        tile, tile, P("img", None, None), vector, vector, matrix, vector, vector, P(), P(),
        matrix, vector, vector, vector, matrix, vector, matrix, vector,
    )
    out_specs = (
        tile, tile, vector, vector, matrix, vector, vector, P(), P(),
        matrix, vector, vector, vector, matrix, vector, matrix, vector,
    )
    return jax.shard_map(body, mesh=mesh, in_specs=in_specs, out_specs=out_specs, check_vma=False)
```

time: 2290 us -> 341 us (0.15)
  local copies, waits for them, and re-layouts: 1300 us -> 23.7 us
  matrix products: 384 us -> 0.76 us
  other arithmetic: 378 us -> 3.1 us
  Pallas kernels: 0 us -> 310 us
  blocking collectives: 126 us -> 0 us
  waiting for transfers between devices: 30.3 us -> 0 us
  starting transfers between devices: 30.2 us -> 0 us
    reshape x8 -> x7, local copies, waits for them, and re-layouts: 554 us -> 2.43 us  [the longest x2 0.82 us: body(): lists[:, :8 * piece].reshape(devices, 8, piece).transpose(1, 0, 2)]
    dot_general x26 -> x4, matrix products: 384 us -> 0.76 us  [the longest x2 0.39 us: rel_tables(): jnp.einsum('mc,ml->cl', table, select[0].astype(BF16), preferred_element_...]
    pallas_call x0 -> x11, Pallas kernels: none -> 310 us  [the longest x7 100 us: call(): pl.pallas_call(kernel, out_shape=[jax.ShapeDtypeStruct(shape, kind) for s...]
    dynamic_update_slice x36 -> x0, local copies, waits for them, and re-layouts: 213 us -> none  [place_blocks(): lax.dynamic_update_slice(canvas, current + blocks[slot_index], starts)]
    reduce_sum x11 -> x0, other arithmetic: 193 us -> none  [the longest x1 102 us: attend_back(): rows_sum = jnp.sum(grid_scores, axis=5)]
    another operation x98 -> x0, local copies, waits for them, and re-layouts: 137 us -> none  [the longest x38 78.3 us: slot_inputs(): jnp.stack([cut_block(wide_q, entry[0], entry[1]) for entry in slots])]
    unnamed x276 -> x48, local copies, waits for them, and re-layouts: 99.6 us -> 8.58 us
    unnamed x3 -> x0, blocking collectives: 86.3 us -> none
  transfers between devices with their start and end apart: 21 -> 0, of which waited for: 2 -> 0; matrix products, arithmetic and copies ran while one was open for 89% -> 0% of each run, Pallas kernels for 0% -> 0%
where the time goes in v1:
time: 341 us; the launch traced here: 339 us
  Pallas kernels  310 us (91%)
  local copies, waits for them, and re-layouts  23.7 us (7%)
    pallas_call x7, Pallas kernels, call(): pl.pallas_call(kernel, out_shape=[jax.ShapeDtypeStruct(shape, kind) for s...  100 us
    pallas_call x1, Pallas kernels, scatter(): pl.pallas_call(functools.partial(scatter_kernel, groups, term is not None...  93.6 us
    pallas_call x1, Pallas kernels, gather(): pl.pallas_call(functools.partial(gather_kernel, groups), out_shape=[jax.S...  77.1 us
    pallas_call x2, Pallas kernels, move_windows(): pl.pallas_call(kernel, out_shape=[jax.ShapeDtypeStruct((length, D), BF16)...  39.1 us
    unnamed x48, local copies, waits for them, and re-layouts  8.58 us

profile of v1, /device:TPU:0, one launch (start us, length us, event | category | flops | bytes accessed | tf_op | source)
XLA Modules:
  0.0 338.7 jit_solution(7879152545797179771)
XLA Ops:
  0.7 0.0 copy-start
  0.7 0.0 copy-start.9
  0.7 0.0 copy-start.10
  0.7 0.0 copy-start.11
  0.7 0.0 copy-start.12
  0.7 0.0 copy-start.13
  0.8 0.8 dynamic-slice_bitcast_fusion.3
  1.6 0.8 copy.46.refs_2_
  2.4 0.7 dynamic-slice_bitcast_fusion.1
  3.1 0.9 copy.47.refs_3_
  4.0 21.8 %shard_map.395 = (bf16[624,768]{1,0:T(8,128)(2,1)}, bf16[624,768]{1,0:T(8,128)(2,1)}) custom-call(bf16[512,768]{1,0:T(8,128)(2,1)} %bitcast.60, bf16[512,768]{1,0:T(8,128)(2,1)} %bitcast.61, s32[384,1]{1,0:T(8,128)} %copy.46.refs_2_, s32[624,1]{1,0:T(8,128)} %copy.47.refs_3_), custom_call_target="tpu_custom_call" | custom-call | tf_op jit(solution)/shard_map/pallas_call | solution.py:864
  25.8 1.7 dynamic-slice_bitcast_fusion.where_ref
  27.5 0.0 copy-done.10
  27.6 0.1 concatenate.17
  27.7 0.6 pad_bitcast_fusion.refs_0_
  28.3 77.1 %shard_map.396 = (bf16[2,2,2,4,16,128]{5,4,3,2,1,0:T(8,128)(2,1)}, bf16[2,2,2,4,24,2304]{5,4,3,2,1,0:T(8,128)(2,1)}, bf16[2,2,2,4,24,768]{5,4,3,2,1,0:T(8,128)(2...) custom-call(bf16[16,128]{1,0:T(8,128)(2,1)} %pad_bitcast_fusion.refs_0_, ...), custom_call_target="tpu_custom_call" | custom-call | tf_op jit(solution)/shard_map/pallas_call | solution.py:599
  105.4 0.9 copy.55
  106.3 0.0 copy-start.19
  106.3 0.0 copy-start.18
  106.4 0.1 reshape.109
  106.5 0.7 reshape.110.vec_ref
  107.2 0.0 copy-done.6
  107.2 0.6 convert_bitcast_fusion.mask_ref
  107.8 7.0 %shard_map.397 = (bf16[624,768]{1,0:T(8,128)(2,1)}, bf16[624,2304]{1,0:T(8,128)(2,1)}, bf16[624,128]{1,0:T(8,128)(2,1)}) custom-call(bf16[624,768]{1,0:T(8,128)(2,1)} %get-tuple-element.55.x_ref, f32[8,768]{1,0:T(8,128)} %reshape.110.vec_ref, bf16[64,64]{1,0:T(8,128)(2,1)} %convert_bitcast_fusion.mask_ref, s32[624,8]{1,0:T(8,128)} %dynamic-slice_bitcast_fusion.where_ref, ...), custom_call_target="tpu_custom_call" | custom-call | tf_op jit(solution)/shard_map/pallas_call | solution.py:369
  114.8 0.0 copy-done.19
  114.8 0.2 fusion
  115.0 0.0 copy-done.18
  115.0 0.2 fusion.1
  115.2 0.7 maximum_maximum_fusion.rel_ref
  115.9 21.5 %shard_map.398 = (bf16[624,768]{1,0:T(8,128)(2,1)}, bf16[3,6,416,208]{3,2,1,0:T(8,128)(2,1)}) custom-call(bf16[624,2304]{1,0:T(8,128)(2,1)} %get-tuple-element.58.q_ref.k_ref.v_ref, bf16[624,2304]{1,0:T(8,128)(2,1)} %get-tuple-element.58.q_ref.k_ref.v_ref, bf16[624,2304]{1,0:T(8,128)(2,1)} %get-tuple-element.58.q_ref.k_ref.v_ref, ...), custom_call_target="tpu_custom_call" | custom-call | tf_op jit(solution)/shard_map/pallas_call | solution.py:369
  137.4 4.5 %shard_map.399 = (f32[624,768]{1,0:T(8,128)}, bf16[624,768]{1,0:T(8,128)(2,1)}) custom-call(bf16[624,768]{1,0:T(8,128)(2,1)} %get-tuple-element.60.o_ref, bf16[624,768]{1,0:T(8,128)(2,1)} %get-tuple-element.55.x_ref, f32[8,768]{1,0:T(8,128)} %reshape.110.vec_ref, bf16[768,768]{1,0:T(8,128)(2,1)} %bitcast.52), custom_call_target="tpu_custom_call" | custom-call | tf_op jit(solution)/shard_map/pallas_call | solution.py:369
  141.9 0.1 slice.96
  142.0 0.7 reshape.113.b1_ref
  142.6 27.3 %shard_map.400 = (bf16[624,768]{1,0:T(8,128)(2,1)}, f32[624,768]{1,0:T(8,128)}, bf16[768,3072]{1,0:T(8,128)(2,1)}, bf16[3072,768]{1,0:T(8,128)(2,1)}, f32[1,3072]{1,0:T(1,128)}) custom-call(bf16[624,768]{1,0:T(8,128)(2,1)} %get-tuple-element.62.n2_ref, bf16[624,768]{1,0:T(8,128)(2,1)} %get-tuple-element.63.g_ref, f32[624,768]{1,0:T(8,128)} %get-tuple-element.64.r_ref, ...), custom_call_target="tpu_custom_call" | custom-call | tf_op jit(solution)/shard_map/pallas_call | solution.py:369
  170.0 7.4 %shard_map.401 = (f32[624,768]{1,0:T(8,128)}, bf16[624,768]{1,0:T(8,128)(2,1)}, bf16[768,768]{1,0:T(8,128)(2,1)}, f32[8,768]{1,0:T(8,128)}) custom-call(f32[624,768]{1,0:T(8,128)} %get-tuple-element.68.dn2_ref, f32[624,768]{1,0:T(8,128)} %get-tuple-element.64.r_ref, bf16[624,768]{1,0:T(8,128)(2,1)} %get-tuple-element.63.g_ref, ...), custom_call_target="tpu_custom_call" | custom-call | tf_op jit(solution)/shard_map/pallas_call | solution.py:369
  177.4 21.2 %shard_map.402 = (bf16[624,768]{1,0:T(8,128)(2,1)}, bf16[624,768]{1,0:T(8,128)(2,1)}, bf16[624,768]{1,0:T(8,128)(2,1)}, f32[128,512]{1,0:T(8,128)}) custom-call(bf16[624,2304]{1,0:T(8,128)(2,1)} %get-tuple-element.58.q_ref.k_ref.v_ref, bf16[624,2304]{1,0:T(8,128)(2,1)} %get-tuple-element.58.q_ref.k_ref.v_ref, ...), custom_call_target="tpu_custom_call" | custom-call | tf_op jit(solution)/shard_map/pallas_call | solution.py:369
  198.6 1.0 slice_add_fusion
  199.6 0.2 fusion.6
  199.8 0.2 fusion.8
  199.9 0.7 select_maximum_fusion.refs_5_
  200.6 11.5 %shard_map.403 = (bf16[624,768]{1,0:T(8,128)(2,1)}, bf16[768,2304]{1,0:T(8,128)(2,1)}, f32[8,768]{1,0:T(8,128)}) custom-call(bf16[624,768]{1,0:T(8,128)(2,1)} %get-tuple-element.71.dq_ref, bf16[624,768]{1,0:T(8,128)(2,1)} %get-tuple-element.72.dk_ref, bf16[624,768]{1,0:T(8,128)(2,1)} %get-tuple-element.73.dv_ref, bf16[624,768]{1,0:T(8,128)(2,1)} %get-tuple-element.74.n1_ref, ...), custom_call_target="tpu_custom_call" | custom-call | tf_op jit(solution)/shard_map/pallas_call | solution.py:369
  212.1 0.7 slice.119
  212.9 0.1 reshape.118
  213.1 0.1 reshape.119
  213.2 0.0 copy-done.8
  213.2 0.1 reshape.120
  213.3 0.1 fusion.5
  213.4 0.7 copy.53
  214.1 93.6 %shard_map.405 = (f32[16,128]{1,0:T(8,128)}, f32[24,2304]{1,0:T(8,128)}, f32[24,768]{1,0:T(8,128)}, f32[24,3072]{1,0:T(8,128)}, f32[96,768]{1,0:T(8,128)}, /*index=5*/f32[32,128]{1,0:T(8,128)}) custom-call(bf16[2,2,2,4,16,128]{5,4,3,2,1,0:T(8,128)(2,1)} %bitcast.62, bf16[2,2,2,4,24,2304]{5,4,3,2,1,0:T(8,128)(2,1)} %bitcast.56, ...), custom_call_target="tpu_custom_call" | custom-call | tf_op jit(solution)/shard_map/pallas_call | solution.py:786
  307.7 1.5 fusion.10
  309.2 1.6 fusion.11
  310.8 1.3 slice.109
  312.0 0.8 copy.49.refs_2_
  312.9 0.7 dynamic-slice_bitcast_fusion.2
  313.6 0.9 copy.50.refs_3_
  314.5 17.4 %shard_map.404 = (bf16[512,768]{1,0:T(8,128)(2,1)}, bf16[512,768]{1,0:T(8,128)(2,1)}) custom-call(bf16[624,768]{1,0:T(8,128)(2,1)} %get-tuple-element.67.refs_0_, bf16[624,768]{1,0:T(8,128)(2,1)} %get-tuple-element.76.refs_1_, s32[384,1]{1,0:T(8,128)} %copy.49.refs_2_, s32[512,1]{1,0:T(8,128)} %copy.50.refs_3_), custom_call_target="tpu_custom_call" | custom-call | tf_op jit(solution)/shard_map/pallas_call | solution.py:864
  331.8 2.1 copy.62
  333.9 2.1 copy.63
  336.0 0.0 copy-done.3
  336.0 0.7 copy.64
  336.6 0.0 copy-done.5
  336.6 0.6 copy.65
  337.3 0.7 copy.66
  338.0 0.7 copy.67
  (34 shorter events, 0.2 us)
Async XLA Ops:
  0.7 114.2 %copy-start = (bf16[27,64]{1,0:T(8,128)(2,1)S(1)}, bf16[27,64]{1,0:T(8,128)(2,1)}, u32[]{:S(2)}) copy-start(bf16[27,64]{1,0:T(8,128)(2,1)} %param.36) | copy-start | bytes 10372
  0.7 26.9 %copy-start.9 = (bf16[24]{0:T(256)(128)(2,1)S(1)}, bf16[24]{0:T(256)(128)(2,1)}, u32[]{:S(2)}) copy-start(bf16[24]{0:T(256)(128)(2,1)} %param.31) | copy-start | bytes 148
  0.7 26.8 %copy-start.10 = (bf16[24]{0:T(256)(128)(2,1)S(1)}, bf16[24]{0:T(256)(128)(2,1)}, u32[]{:S(2)}) copy-start(bf16[24]{0:T(256)(128)(2,1)} %param.32) | copy-start | bytes 148
  0.7 26.8 %copy-start.11 = (bf16[24]{0:T(256)(128)(2,1)S(1)}, bf16[24]{0:T(256)(128)(2,1)}, u32[]{:S(2)}) copy-start(bf16[24]{0:T(256)(128)(2,1)} %param.34) | copy-start | bytes 148
  0.7 26.8 %copy-start.12 = (bf16[24]{0:T(256)(128)(2,1)S(1)}, bf16[24]{0:T(256)(128)(2,1)}, u32[]{:S(2)}) copy-start(bf16[24]{0:T(256)(128)(2,1)} %param.35) | copy-start | bytes 148
  0.7 26.8 %copy-start.13 = (bf16[24]{0:T(256)(128)(2,1)S(1)}, bf16[24]{0:T(256)(128)(2,1)}, u32[]{:S(2)}) copy-start(bf16[24]{0:T(256)(128)(2,1)} %param.39) | copy-start | bytes 148
  0.7 26.8 %copy-start.14 = (bf16[24]{0:T(256)(128)(2,1)S(1)}, bf16[24]{0:T(256)(128)(2,1)}, u32[]{:S(2)}) copy-start(bf16[24]{0:T(256)(128)(2,1)} %param.40) | copy-start | bytes 148
  0.7 26.8 %copy-start.15 = (bf16[24]{0:T(256)(128)(2,1)S(1)}, bf16[24]{0:T(256)(128)(2,1)}, u32[]{:S(2)}) copy-start(bf16[24]{0:T(256)(128)(2,1)} %param.41) | copy-start | bytes 148
  0.7 26.8 %copy-start.17 = (bf16[96]{0:T(256)(128)(2,1)S(1)}, bf16[96]{0:T(256)(128)(2,1)}, u32[]{:S(2)}) copy-start(bf16[96]{0:T(256)(128)(2,1)} %param.43) | copy-start | bytes 580
  0.8 26.8 %copy-start.16 = (bf16[24]{0:T(256)(128)(2,1)S(1)}, bf16[24]{0:T(256)(128)(2,1)}, u32[]{:S(2)}) copy-start(bf16[24]{0:T(256)(128)(2,1)} %param.45) | copy-start | bytes 148
  0.8 106.5 %copy-start.6 = (s32[1,64,64]{2,1,0:T(8,128)S(1)}, s32[1,64,64]{2,1,0:T(8,128)}, u32[]{:S(2)}) copy-start(s32[1,64,64]{2,1,0:T(8,128)} %param.30) | copy-start | bytes 49156
  106.3 8.5 %copy-start.19 = (bf16[27,256]{1,0:T(8,128)(2,1)S(1)}, bf16[27,256]{1,0:T(8,128)(2,1)}, u32[]{:S(2)}) copy-start(bf16[27,256]{1,0:T(8,128)(2,1)} %constant.57.clone) | copy-start | bytes 41476
  106.3 8.7 %copy-start.18 = (bf16[27,64]{1,0:T(8,128)(2,1)S(1)}, bf16[27,64]{1,0:T(8,128)(2,1)}, u32[]{:S(2)}) copy-start(bf16[27,64]{1,0:T(8,128)(2,1)} %param.37) | copy-start | bytes 10372
  177.4 22.2 %copy-start.4 = (f32[27,256]{1,0:T(8,128)S(1)}, f32[27,256]{1,0:T(8,128)}, u32[]{:S(2)}) copy-start(f32[27,256]{1,0:T(8,128)} %constant.59.clone) | copy-start | bytes 82948
  200.6 12.2 %copy-start.7 = (f32[8,768]{1,0:T(8,128)S(1)}, f32[8,768]{1,0:T(8,128)}, u32[]{:S(2)}) copy-start(f32[8,768]{1,0:T(8,128)} %get-tuple-element.80) | copy-start | bytes 73732
  200.6 12.6 %copy-start.8 = (f32[1,3072]{1,0:T(1,128)S(1)}, f32[1,3072]{1,0:T(1,128)}, u32[]{:S(2)}) copy-start(f32[1,3072]{1,0:T(1,128)} %get-tuple-element.81) | copy-start | bytes 36868
  313.6 22.4 %copy-start.3 = (f32[24,2304]{1,0:T(8,128)S(1)}, f32[24,2304]{1,0:T(8,128)}, u32[]{:S(2)}) copy-start(f32[24,2304]{1,0:T(8,128)} %get-tuple-element.126) | copy-start | bytes 663556
  314.5 22.2 %copy-start.5 = (f32[24,768]{1,0:T(8,128)S(1)}, f32[24,768]{1,0:T(8,128)}, u32[]{:S(2)}) copy-start(f32[24,768]{1,0:T(8,128)} %get-tuple-element.131) | copy-start | bytes 221188
  314.5 22.8 %copy-start.2 = (f32[24,3072]{1,0:T(8,128)S(1)}, f32[24,3072]{1,0:T(8,128)}, u32[]{:S(2)}) copy-start(f32[24,3072]{1,0:T(8,128)} %get-tuple-element.135) | copy-start | bytes 884740
  314.5 23.5 %copy-start.1 = (f32[96,768]{1,0:T(8,128)S(1)}, f32[96,768]{1,0:T(8,128)}, u32[]{:S(2)}) copy-start(f32[96,768]{1,0:T(8,128)} %get-tuple-element.137) | copy-start | bytes 884740
